TPU v7x, 32 devices: a whole 2x2x4 slice. The times are simulated.
32 devices in a mesh: wide: 8 (over y, x, core), narrow: 4 (over z).
Axes of the slice: x: 2, y: 2, z: 4, core: 2. Of those that a mesh axis runs over, the one named last changes fastest.
Arguments:
- source: bfloat16 [32, 1024, 512], P(('wide', 'narrow')), may hold values from -6 to 6
- target: bfloat16 [32, 1024, 512], P(('wide', 'narrow')), may hold values from -6 to 6
- source_segments: int32 [32, 1024], P(('wide', 'narrow')), may hold values from -1 to 773, as said below
- target_segments: int32 [32, 1024], P(('wide', 'narrow')), may hold values from -1 to 773, as said below
- encoder_proj: bfloat16 [3, 512, 512], P(None, ('wide', 'narrow')), may hold values from -0.25 to 0.25
- encoder_mix: bfloat16 [512, 512], P(('wide', 'narrow')), may hold values from -1 to 1
- encoder_up: bfloat16 [512, 2048], P(('wide', 'narrow')), may hold values from -0.25 to 0.25
- encoder_down: bfloat16 [2048, 512], P(('wide', 'narrow')), may hold values from -0.125 to 0.125
- self_proj: bfloat16 [3, 512, 512], P(None, ('wide', 'narrow')), may hold values from -0.25 to 0.25
- self_mix: bfloat16 [512, 512], P(('wide', 'narrow')), may hold values from -1 to 1
- cross_proj: bfloat16 [3, 512, 512], P(None, ('wide', 'narrow')), may hold values from -0.25 to 0.25
- cross_mix: bfloat16 [512, 512], P(('wide', 'narrow')), may hold values from -1 to 1
- decoder_up: bfloat16 [512, 2048], P(('wide', 'narrow')), may hold values from -0.25 to 0.25
- decoder_down: bfloat16 [2048, 512], P(('wide', 'narrow')), may hold values from -0.125 to 0.125
- norm_gain: bfloat16 [5, 512], P(None, ('wide', 'narrow')), may hold values from 0.5 to 1.5
- norm_bias: bfloat16 [5, 512], P(None, ('wide', 'narrow')), may hold values from -1.5 to 1.5
- cotangent: bfloat16 [32, 1024, 512], P(('wide', 'narrow')), may hold values from -6 to 6
Outputs:
- decoded: bfloat16 [32, 1024, 512], P(('wide', 'narrow'))
- source_grad: bfloat16 [32, 1024, 512], P(('wide', 'narrow'))
- target_grad: bfloat16 [32, 1024, 512], P(('wide', 'narrow'))
- encoder_proj_grad: float32 [3, 512, 512], P(None, ('wide', 'narrow'))
- encoder_mix_grad: float32 [512, 512], P(('wide', 'narrow'))
- encoder_up_grad: float32 [512, 2048], P(('wide', 'narrow'))
- encoder_down_grad: float32 [2048, 512], P(('wide', 'narrow'))
- self_proj_grad: float32 [3, 512, 512], P(None, ('wide', 'narrow'))
- self_mix_grad: float32 [512, 512], P(('wide', 'narrow'))
- cross_proj_grad: float32 [3, 512, 512], P(None, ('wide', 'narrow'))
- cross_mix_grad: float32 [512, 512], P(('wide', 'narrow'))
- decoder_up_grad: float32 [512, 2048], P(('wide', 'narrow'))
- decoder_down_grad: float32 [2048, 512], P(('wide', 'narrow'))
- norm_gain_grad: float32 [5, 512], P(None, ('wide', 'narrow'))
- norm_bias_grad: float32 [5, 512], P(None, ('wide', 'narrow'))
Inputs may be any that keep to these rules, and one draw needn't show every extreme that they name: `source_segments`: source sentence k and target sentence k of the same row are a translation pair; in each row sentence numbers start at 0 and rise by one, both rows of a pair hold the same number of sentences, and -1 marks the padding at the end of each row (at least one position). Each sentence has 1 to 250 tokens, and one sentence of each row has exactly 250. `target_segments`: as for source_segments: the pairs of sentences match by number, -1 marks the padding at the end of each row, and one sentence of each row has exactly 250 tokens.
All inputs are finite; a program needn't handle non-finite values.
Results may differ from a plain program's by a relative error of at most 0.024.
Values may be sent and summed in bfloat16 or wider, within the bound.
No kernel may reach another device: no remote copies, remote signals or barrier semaphores. Data moves between devices by JAX's collectives and lax.ppermute only.
A program may use at most 256 MiB of HBM per device.

v0:
```python
from functools import partial

import jax
import jax.numpy as jnp
from jax import lax
from jax.sharding import PartitionSpec as P

HEADS = 8


norm_eps = 1e-05
masked_score = -1e30


def project(left, weight):
    return jnp.dot(left, weight, preferred_element_type=jnp.float32)


def project_back(grad, weight):
    return jnp.einsum("nf,df->nd", grad, weight, preferred_element_type=jnp.float32)


def outer_sum(left, grad):
    return jnp.einsum("nd,nf->df", left, grad, preferred_element_type=jnp.float32)


def layer_norm(resid, gain, bias):
    mean = jnp.mean(resid, axis=-1, keepdims=True)
    centred = resid - mean
    scale_inv = lax.rsqrt(jnp.mean(centred * centred, axis=-1, keepdims=True) + norm_eps)
    normed = centred * scale_inv
    return (normed * gain + bias, (normed, scale_inv))


def layer_norm_back(grad, saved, gain):
    normed, scale_inv = saved
    scaled = grad * gain
    mean_plain = jnp.mean(scaled, axis=-1, keepdims=True)
    mean_normed = jnp.mean(scaled * normed, axis=-1, keepdims=True)
    grad_resid = scale_inv * (scaled - mean_plain - normed * mean_normed)
    return (grad_resid, jnp.sum(grad * normed, axis=0), jnp.sum(grad, axis=0))


def allowed_keys(query_segments, key_segments, start, causal):
    allowed = query_segments[:, None] == key_segments[None, :]
    if causal:
        query_place = start + lax.broadcasted_iota(jnp.int32, allowed.shape, 0)
        key_place = lax.broadcasted_iota(jnp.int32, allowed.shape, 1)
        allowed = allowed & (query_place >= key_place)
    return allowed


def block_scores(query_block, key_row, allowed, scale):
    scores = (
        jnp.einsum("qhd,khd->hqk", query_block, key_row, preferred_element_type=jnp.float32) * scale
    )
    return jnp.where(allowed[None], scores, masked_score)


def block_layout(query, query_segments):
    rows, length = query_segments.shape
    block = min(512, length)
    count = length // block
    width = query.shape[-1] // HEADS
    return (rows, block, count, width)


def attend_forward(query, key, value, query_segments, key_segments, causal):
    rows, block, count, width = block_layout(query, query_segments)
    scale = width ** (-0.5)
    key_rows = key.reshape(rows, -1, HEADS, width)
    value_rows = value.reshape(rows, -1, HEADS, width)
    query_blocks = query.reshape(rows * count, block, HEADS, width)
    segment_blocks = query_segments.reshape(rows * count, block)

    def one_block(items):
        index, query_block, segment_block = items
        row = index // count
        start = index % count * block
        key_row = lax.dynamic_index_in_dim(key_rows, row, 0, keepdims=False)
        value_row = lax.dynamic_index_in_dim(value_rows, row, 0, keepdims=False)
        key_segment = lax.dynamic_index_in_dim(key_segments, row, 0, keepdims=False)
        scores = block_scores(
            query_block, key_row, allowed_keys(segment_block, key_segment, start, causal), scale
        )
        peak = jnp.max(scores, axis=-1, keepdims=True)
        total = peak + jnp.log(jnp.sum(jnp.exp(scores - peak), axis=-1, keepdims=True))
        probs = jnp.exp(scores - total).astype(jnp.bfloat16)
        mixed = jnp.einsum("hqk,khd->qhd", probs, value_row, preferred_element_type=jnp.float32)
        return (mixed.astype(jnp.bfloat16), total[..., 0])

    indices = jnp.arange(rows * count, dtype=jnp.int32)
    mixed, totals = lax.map(one_block, (indices, query_blocks, segment_blocks))
    return (mixed.reshape(query.shape), totals)


def attend_backward(query, key, value, query_segments, key_segments, causal, totals, grad_mixed):
    rows, block, count, width = block_layout(query, query_segments)
    scale = width ** (-0.5)
    key_length = key.shape[0] // rows
    key_rows = key.reshape(rows, key_length, HEADS, width)
    value_rows = value.reshape(rows, key_length, HEADS, width)
    query_blocks = query.reshape(rows * count, block, HEADS, width)
    grad_blocks = grad_mixed.reshape(rows * count, block, HEADS, width)
    segment_blocks = query_segments.reshape(rows * count, block)

    def one_block(items):
        index, query_block, segment_block, total, grad_block = items
        row = index // count
        start = index % count * block
        key_row = lax.dynamic_index_in_dim(key_rows, row, 0, keepdims=False)
        value_row = lax.dynamic_index_in_dim(value_rows, row, 0, keepdims=False)
        key_segment = lax.dynamic_index_in_dim(key_segments, row, 0, keepdims=False)
        scores = block_scores(
            query_block, key_row, allowed_keys(segment_block, key_segment, start, causal), scale
        )
        probs = jnp.exp(scores - total[..., None])
        grad_probs = jnp.einsum(
            "qhd,khd->hqk", grad_block, value_row, preferred_element_type=jnp.float32
        )
        inner = jnp.sum(probs * grad_probs, axis=-1, keepdims=True)
        grad_scores = (probs * (grad_probs - inner)).astype(jnp.bfloat16)
        grad_query = (
            jnp.einsum("hqk,khd->qhd", grad_scores, key_row, preferred_element_type=jnp.float32)
            * scale
        )
        grad_key = (
            jnp.einsum("hqk,qhd->khd", grad_scores, query_block, preferred_element_type=jnp.float32)
            * scale
        )
        grad_value = jnp.einsum(
            "hqk,qhd->khd",
            probs.astype(jnp.bfloat16),
            grad_block,
            preferred_element_type=jnp.float32,
        )
        return (grad_query.astype(jnp.bfloat16), grad_key, grad_value)

    indices = jnp.arange(rows * count, dtype=jnp.int32)
    grad_query, grad_key, grad_value = lax.map(
        one_block, (indices, query_blocks, segment_blocks, totals, grad_blocks)
    )
    grad_key = jnp.sum(grad_key.reshape(rows, count, key_length, HEADS * width), axis=1)
    grad_value = jnp.sum(grad_value.reshape(rows, count, key_length, HEADS * width), axis=1)
    return (
        grad_query.reshape(query.shape),
        grad_key.reshape(key.shape).astype(jnp.bfloat16),
        grad_value.reshape(value.shape).astype(jnp.bfloat16),
    )


def attention_forward(query_in, source_in, weights, mix, query_segments, key_segments, causal):
    query = project(query_in, weights[0]).astype(jnp.bfloat16)
    key = project(source_in, weights[1]).astype(jnp.bfloat16)
    value = project(source_in, weights[2]).astype(jnp.bfloat16)
    mixed, totals = attend_forward(query, key, value, query_segments, key_segments, causal)
    return (project(mixed, mix), (query, key, value, mixed, totals))


def attention_backward(
    grad, query_in, source_in, weights, mix, saved, query_segments, key_segments, causal
):
    query, key, value, mixed, totals = saved
    grad_low = grad.astype(jnp.bfloat16)
    mix_grad = outer_sum(mixed, grad_low)
    grad_mixed = project_back(grad_low, mix).astype(jnp.bfloat16)
    grad_query, grad_key, grad_value = attend_backward(
        query, key, value, query_segments, key_segments, causal, totals, grad_mixed
    )
    proj_grad = jnp.stack(
        [
            outer_sum(query_in, grad_query),
            outer_sum(source_in, grad_key),
            outer_sum(source_in, grad_value),
        ]
    )
    query_side = project_back(grad_query, weights[0])
    source_side = project_back(grad_key, weights[1]) + project_back(grad_value, weights[2])
    return (query_side, source_side, proj_grad, mix_grad)


def ffn_forward(normed_in, up_weight, down_weight):
    hidden_pre = project(normed_in, up_weight)
    active = jax.nn.gelu(hidden_pre, approximate=True).astype(jnp.bfloat16)
    return (project(active, down_weight), (hidden_pre, active))


def ffn_backward(grad, normed_in, up_weight, down_weight, saved):
    hidden_pre, active = saved
    grad_low = grad.astype(jnp.bfloat16)
    down_grad = outer_sum(active, grad_low)
    grad_active = project_back(grad_low, down_weight)
    unused, pullback = jax.vjp(partial(jax.nn.gelu, approximate=True), hidden_pre)
    grad_hidden = pullback(grad_active)[0].astype(jnp.bfloat16)
    up_grad = outer_sum(normed_in, grad_hidden)
    return (project_back(grad_hidden, up_weight), up_grad, down_grad)


def fetch_attention(proj_shard, mix_shard):
    return (
        lax.all_gather(proj_shard, ("wide", "narrow"), axis=1, tiled=True),
        lax.all_gather(mix_shard, ("wide", "narrow"), axis=0, tiled=True),
    )


def fetch_ffn(up_shard, down_shard):
    return (
        lax.all_gather(up_shard, ("wide", "narrow"), axis=0, tiled=True),
        lax.all_gather(down_shard, ("wide", "narrow"), axis=0, tiled=True),
    )


def attention_again(proj_shard, mix_shard):
    return (
        lax.all_gather(proj_shard, ("wide", "narrow"), axis=1, tiled=True),
        lax.all_gather(mix_shard, ("wide", "narrow"), axis=0, tiled=True),
    )


def ffn_again(up_shard, down_shard):
    return (
        lax.all_gather(up_shard, ("wide", "narrow"), axis=0, tiled=True),
        lax.all_gather(down_shard, ("wide", "narrow"), axis=0, tiled=True),
    )


def reduce_attention(proj_grad, mix_grad):
    return (
        lax.psum_scatter(proj_grad, ("wide", "narrow"), scatter_dimension=1, tiled=True),
        lax.psum_scatter(mix_grad, ("wide", "narrow"), scatter_dimension=0, tiled=True),
    )


def reduce_ffn(up_grad, down_grad):
    return (
        lax.psum_scatter(up_grad, ("wide", "narrow"), scatter_dimension=0, tiled=True),
        lax.psum_scatter(down_grad, ("wide", "narrow"), scatter_dimension=0, tiled=True),
    )


def on_device(
    source,
    target,
    source_segments,
    target_segments,
    encoder_proj,
    encoder_mix,
    encoder_up,
    encoder_down,
    self_proj,
    self_mix,
    cross_proj,
    cross_mix,
    decoder_up,
    decoder_down,
    norm_gain,
    norm_bias,
    cotangent,
):
    width = source.shape[-1]
    source_low = source.reshape(-1, width)
    target_low = target.reshape(-1, width)
    enc_proj_all, enc_mix_all, gain_all, bias_all = (
        lax.all_gather(encoder_proj, ("wide", "narrow"), axis=1, tiled=True),
        lax.all_gather(encoder_mix, ("wide", "narrow"), axis=0, tiled=True),
        lax.all_gather(norm_gain, ("wide", "narrow"), axis=1, tiled=True),
        lax.all_gather(norm_bias, ("wide", "narrow"), axis=1, tiled=True),
    )
    gains = gain_all.astype(jnp.float32)
    biases = bias_all.astype(jnp.float32)
    branch, enc_attn_saved = attention_forward(
        source_low, source_low, enc_proj_all, enc_mix_all, source_segments, source_segments, False
    )
    first, norm_first = layer_norm(source_low.astype(jnp.float32) + branch, gains[0], biases[0])
    first_low = first.astype(jnp.bfloat16)
    enc_ffn_all = fetch_ffn(encoder_up, encoder_down)
    branch, enc_ffn_saved = ffn_forward(first_low, enc_ffn_all[0], enc_ffn_all[1])
    encoded, norm_encoded = layer_norm(first + branch, gains[1], biases[1])
    encoded_low = encoded.astype(jnp.bfloat16)
    self_all = fetch_attention(self_proj, self_mix)
    branch, self_saved = attention_forward(
        target_low, target_low, self_all[0], self_all[1], target_segments, target_segments, True
    )
    second, norm_second = layer_norm(target_low.astype(jnp.float32) + branch, gains[2], biases[2])
    second_low = second.astype(jnp.bfloat16)
    cross_all = fetch_attention(cross_proj, cross_mix)
    branch, cross_saved = attention_forward(
        second_low, encoded_low, cross_all[0], cross_all[1], target_segments, source_segments, False
    )
    third, norm_third = layer_norm(second + branch, gains[3], biases[3])
    third_low = third.astype(jnp.bfloat16)
    dec_ffn_all = fetch_ffn(decoder_up, decoder_down)
    branch, dec_ffn_saved = ffn_forward(third_low, dec_ffn_all[0], dec_ffn_all[1])
    final, norm_final = layer_norm(third + branch, gains[4], biases[4])
    valid = (target_segments >= 0).reshape(-1, 1).astype(jnp.float32)
    grad_final = cotangent.reshape(-1, width).astype(jnp.float32) * valid
    grad_resid, gain_four, bias_four = layer_norm_back(grad_final, norm_final, gains[4])
    dec_ffn_back = ffn_again(decoder_up, decoder_down)
    grad_input, up_grad, down_grad = ffn_backward(
        grad_resid, third_low, dec_ffn_back[0], dec_ffn_back[1], dec_ffn_saved
    )
    dec_up_grad, dec_down_grad = reduce_ffn(up_grad, down_grad)
    grad_resid, gain_three, bias_three = layer_norm_back(
        grad_resid + grad_input, norm_third, gains[3]
    )
    cross_back = attention_again(cross_proj, cross_mix)
    query_side, source_side, proj_grad, mix_grad = attention_backward(
        grad_resid,
        second_low,
        encoded_low,
        cross_back[0],
        cross_back[1],
        cross_saved,
        target_segments,
        source_segments,
        False,
    )
    cross_proj_grad, cross_mix_grad = reduce_attention(proj_grad, mix_grad)
    grad_encoded = source_side
    grad_resid, gain_two, bias_two = layer_norm_back(grad_resid + query_side, norm_second, gains[2])
    self_back = attention_again(self_proj, self_mix)
    query_side, source_side, proj_grad, mix_grad = attention_backward(
        grad_resid,
        target_low,
        target_low,
        self_back[0],
        self_back[1],
        self_saved,
        target_segments,
        target_segments,
        True,
    )
    self_proj_grad, self_mix_grad = reduce_attention(proj_grad, mix_grad)
    target_grad = grad_resid + query_side + source_side
    grad_resid, gain_one, bias_one = layer_norm_back(grad_encoded, norm_encoded, gains[1])
    enc_ffn_back = ffn_again(encoder_up, encoder_down)
    grad_input, up_grad, down_grad = ffn_backward(
        grad_resid, first_low, enc_ffn_back[0], enc_ffn_back[1], enc_ffn_saved
    )
    enc_up_grad, enc_down_grad = reduce_ffn(up_grad, down_grad)
    grad_resid, gain_zero, bias_zero = layer_norm_back(
        grad_resid + grad_input, norm_first, gains[0]
    )
    enc_back = attention_again(encoder_proj, encoder_mix)
    query_side, source_side, proj_grad, mix_grad = attention_backward(
        grad_resid,
        source_low,
        source_low,
        enc_back[0],
        enc_back[1],
        enc_attn_saved,
        source_segments,
        source_segments,
        False,
    )
    source_grad = grad_resid + query_side + source_side
    gain_grad = jnp.stack([gain_zero, gain_one, gain_two, gain_three, gain_four])
    bias_grad = jnp.stack([bias_zero, bias_one, bias_two, bias_three, bias_four])
    enc_proj_grad, enc_mix_grad, gain_shard, bias_shard = (
        lax.psum_scatter(proj_grad, ("wide", "narrow"), scatter_dimension=1, tiled=True),
        lax.psum_scatter(mix_grad, ("wide", "narrow"), scatter_dimension=0, tiled=True),
        lax.psum_scatter(gain_grad, ("wide", "narrow"), scatter_dimension=1, tiled=True),
        lax.psum_scatter(bias_grad, ("wide", "narrow"), scatter_dimension=1, tiled=True),
    )
    return (
        final.reshape(target.shape).astype(jnp.bfloat16),
        source_grad.reshape(source.shape).astype(jnp.bfloat16),
        target_grad.reshape(target.shape).astype(jnp.bfloat16),
        enc_proj_grad,
        enc_mix_grad,
        enc_up_grad,
        enc_down_grad,
        self_proj_grad,
        self_mix_grad,
        cross_proj_grad,
        cross_mix_grad,
        dec_up_grad,
        dec_down_grad,
        gain_shard,
        bias_shard,
    )


def solution(mesh):
    return jax.shard_map(
        on_device,
        mesh=mesh,
        in_specs=(
            P(("wide", "narrow"), None, None),
            P(("wide", "narrow"), None, None),
            P(("wide", "narrow"), None),
            P(("wide", "narrow"), None),
            P(None, ("wide", "narrow"), None),
            P(("wide", "narrow"), None),
            P(("wide", "narrow"), None),
            P(("wide", "narrow"), None),
            P(None, ("wide", "narrow"), None),
            P(("wide", "narrow"), None),
            P(None, ("wide", "narrow"), None),
            P(("wide", "narrow"), None),
            P(("wide", "narrow"), None),
            P(("wide", "narrow"), None),
            P(None, ("wide", "narrow")),
            P(None, ("wide", "narrow")),
            P(("wide", "narrow"), None, None),
        ),
        out_specs=(
            P(("wide", "narrow"), None, None),
            P(("wide", "narrow"), None, None),
            P(("wide", "narrow"), None, None),
            P(None, ("wide", "narrow"), None),
            P(("wide", "narrow"), None),
            P(("wide", "narrow"), None),
            P(("wide", "narrow"), None),
            P(None, ("wide", "narrow"), None),
            P(("wide", "narrow"), None),
            P(None, ("wide", "narrow"), None),
            P(("wide", "narrow"), None),
            P(("wide", "narrow"), None),
            P(("wide", "narrow"), None),
            P(None, ("wide", "narrow")),
            P(None, ("wide", "narrow")),
        ),
        check_vma=False,
    )
```

profile of v0, /device:TPU:0, one launch (start us, length us, event | category | flops | bytes accessed | tf_op | source)
XLA Modules:
  0.0 2389.8 jit_solution(14315778700637800839)
XLA Ops:
  16.5 79.7 %all_gather.52 = bf16[512,512]{1,0:T(8,128)(2,1)} all-gather(bf16[16,512]{1,0:T(8,128)(2,1)} %param.34), channel_id=1, replica_groups=mesh['wide'=8,'narrow'=4] {'wide','narrow'}, dimensions={0}, use_global_device_ids=true | all-gather | bytes 540672 | tf_op jit(solution)/shard_map/all_gather | solution.py:265
  98.5 64.3 %all-gather = bf16[32,16,5]{1,2,0:T(8,128)(2,1)S(1)} all-gather(bf16[1,16,5]{1,2,0:T(8,128)(2,1)S(1)} %bitcast.676), channel_id=1, replica_groups=mesh['wide'=8,'narrow'=4] {'wide','narrow'}, dimensions={0}, use_global_device_ids=true | all-gather | bytes 5280 | tf_op jit(solution)/shard_map/all_gather | solution.py:266
  163.7 66.3 %all-gather.1 = bf16[32,16,5]{1,2,0:T(8,128)(2,1)S(1)} all-gather(bf16[1,16,5]{1,2,0:T(8,128)(2,1)S(1)} %bitcast.677), channel_id=1, replica_groups=mesh['wide'=8,'narrow'=4] {'wide','narrow'}, dimensions={0}, use_global_device_ids=true | all-gather | bytes 5280 | tf_op jit(solution)/shard_map/all_gather | solution.py:267
  230.9 74.1 %all_gather.47 = bf16[512,512]{1,0:T(8,128)(2,1)} all-gather(bf16[16,512]{1,0:T(8,128)(2,1)S(1)} %copy-done.135), channel_id=1, replica_groups=mesh['wide'=8,'narrow'=4] {'wide','narrow'}, dimensions={0}, use_global_device_ids=true | all-gather | bytes 540672 | tf_op jit(solution)/shard_map/all_gather | solution.py:202
  306.3 76.1 %all_gather.55 = bf16[512,512]{1,0:T(8,128)(2,1)} all-gather(bf16[16,512]{1,0:T(8,128)(2,1)S(1)} %copy-done.136), channel_id=1, replica_groups=mesh['wide'=8,'narrow'=4] {'wide','narrow'}, dimensions={0}, use_global_device_ids=true | all-gather | bytes 540672 | tf_op jit(solution)/shard_map/all_gather | solution.py:202
  393.2 27.1 %while.87 = (s32[]{:T(128)}, bf16[2,512,8,64]{1,3,2,0:T(8,128)(2,1)}, f32[2,8,512]{2,1,0:T(8,128)S(1)}, s32[2,512]{1,0:T(2,128)S(1)}, s32[1,1024]{1,0:T(1,128)S(...) while((s32[]{:T(128)}, ...), condition=%wide.region_9.10_spmd, body=%wide.region_6.9_spmd.sunk | while | flops 1120661504 | bytes 64104612 | solution.py:93
  436.5 32.7 %while.86 = (s32[]{:T(128)}, bf16[2,512,8,64]{1,3,2,0:T(8,128)(2,1)}, f32[2,8,512]{2,1,0:T(8,128)S(1)}, s32[2,512]{1,0:T(2,128)S(1)}, s32[1,1024]{1,0:T(1,128)S(...) while((s32[]{:T(128)}, ...), condition=%wide.region_3.4_spmd, body=%wide.region_0.3_spmd.sunk | while | flops 1121710592 | bytes 64108876 | solution.py:93
  482.3 8.1 fusion.184
  490.4 7.2 fusion.194
  503.4 30.4 %while.88 = (s32[]{:T(128)}, bf16[2,512,8,64]{1,3,2,0:T(8,128)(2,1)}, f32[2,8,512]{2,1,0:T(8,128)S(1)}, s32[2,512]{1,0:T(2,128)S(1)}, s32[1,1024]{1,0:T(1,128)S(...) while((s32[]{:T(128)}, ...), condition=%wide.region_17.18_spmd, body=%wide.region_14.17_spmd.sunk | while | flops 1120661504 | bytes 64105120 | solution.py:93
  539.2 8.2 fusion.180
  547.4 7.4 fusion.196
  559.6 7.6 fusion.126
  586.5 82.3 %while.89 = (s32[]{:T(128)}, bf16[2,512,8,64]{1,3,2,0:T(8,128)(2,1)}, f32[2,1024,8,64]{1,3,2,0:T(8,128)}, f32[2,1024,8,64]{1,3,2,0:T(8,128)}, s32[2,512]{1,0:T(2...) while((s32[]{:T(128)}, ...), condition=%wide.region_28.29_spmd, body=%wide.region_26.28_spmd.sunk | while | flops 2723672064 | bytes 242054928 | solution.py:140
  593.4 11.5 multiply_reduce_fusion.23
  604.9 6.8 multiply_convert_fusion.12
  617.0 7.7 fusion.309
  634.5 11.5 multiply_reduce_fusion.23
  658.1 7.7 fusion.309
  688.4 7.4 fusion.119
  715.7 85.7 %while.91 = (s32[]{:T(128)}, bf16[2,512,8,64]{1,3,2,0:T(8,128)(2,1)}, f32[2,1024,8,64]{1,3,2,0:T(8,128)}, f32[2,1024,8,64]{1,3,2,0:T(8,128)}, s32[2,512]{1,0:T(2...) while((s32[]{:T(128)}, ...), condition=%wide.region_44.45_spmd, body=%wide.region_42.44_spmd.sunk | while | flops 2724721152 | bytes 246122416 | solution.py:140
  724.1 11.5 multiply_reduce_fusion.25
  735.6 6.9 multiply_convert_fusion.14
  747.8 7.7 fusion.330
  766.7 11.5 multiply_reduce_fusion.25
  778.2 6.9 multiply_convert_fusion.14
  790.4 7.8 fusion.330
  830.3 80.0 %while.90 = (s32[]{:T(128)}, bf16[2,512,8,64]{1,3,2,0:T(8,128)(2,1)}, f32[2,1024,8,64]{1,3,2,0:T(8,128)}, f32[2,1024,8,64]{1,3,2,0:T(8,128)}, s32[2,512]{1,0:T(2...) while((s32[]{:T(128)}, ...), condition=%wide.region_37.38_spmd, body=%wide.region_35.37_spmd.sunk | while | flops 2723672064 | bytes 246118160 | solution.py:140
  836.0 11.5 multiply_reduce_fusion.24
  847.5 6.9 multiply_convert_fusion.13
  859.7 7.7 fusion.319
  875.8 11.5 multiply_reduce_fusion.24
  887.3 6.9 multiply_convert_fusion.13
  899.5 7.7 fusion.319
  958.4 10.6 fusion.170
  969.6 7.3 fusion.178
  977.6 7.3 fusion.182
  985.3 9.9 fusion.164
  1010.3 45.0 %reduce-scatter.31.cloned.1.call-done = f32[16,5]{1,0:T(8,128)} async-done(((f32[512,5]{1,0:T(8,128)}), f32[16,5]{1,0:T(8,128)}) %reduce-scatter.31.cloned.1.call-update) | async-done | bytes 336
  1056.6 179.9 %all-reduce.5.cloned.1.call-done = (f32[3,512,512]{2,0,1:T(4,128)}, f32[3,512,512]{2,0,1:T(4,128)}) async-done(((f32[3,512,512]{2,0,1:T(4,128)}, f32[3,512,512]{2,0,1:T(4,128)}), (f32[3,512,512]{2,0,1:T(4,128)}, f32[3,512,512]{2,0,1:T(4,128)})) %all-reduce.5.cloned.1.call-update) | async-done | bytes 6291472
  1239.7 135.0 %reduce-scatter.21.cloned.1.call-done = f32[16,512]{1,0:T(8,128)} async-done(((f32[512,512]{1,0:T(8,128)}), f32[16,512]{1,0:T(8,128)}) %reduce-scatter.21.cloned.1.call-update) | async-done | bytes 32784 | tf_op jit(solution)/shard_map/reduce_scatter | solution.py:230
  1374.8 134.9 %reduce-scatter.25.cloned.1.call-done = f32[16,512]{1,0:T(8,128)} async-done(((f32[512,512]{1,0:T(8,128)}), f32[16,512]{1,0:T(8,128)}) %reduce-scatter.25.cloned.1.call-update) | async-done | bytes 32784 | tf_op jit(solution)/shard_map/reduce_scatter | solution.py:230
  1509.6 134.8 %reduce-scatter.15.cloned.1.call-done = f32[16,512]{1,0:T(8,128)} async-done(((f32[512,512]{1,0:T(8,128)}), f32[16,512]{1,0:T(8,128)}) %reduce-scatter.15.cloned.1.call-update) | async-done | bytes 32784 | tf_op jit(solution)/shard_map/reduce_scatter | solution.py:361
  1644.4 140.8 %reduce-scatter.23.cloned.1.call-done = f32[3,16,512]{2,1,0:T(8,128)} async-done(((f32[3,512,512]{2,1,0:T(8,128)}), f32[3,16,512]{2,1,0:T(8,128)}) %reduce-scatter.23.cloned.1.call-update) | async-done | bytes 98320 | tf_op jit(solution)/shard_map/reduce_scatter | solution.py:229
  1785.2 149.3 %reduce-scatter.29.cloned.1.call-done = f32[64,512]{1,0:T(8,128)} async-done(((f32[2048,512]{1,0:T(8,128)}), f32[64,512]{1,0:T(8,128)}) %reduce-scatter.29.cloned.1.call-update) | async-done | bytes 131088 | tf_op jit(solution)/shard_map/reduce_scatter | solution.py:237
  1934.5 149.3 %reduce-scatter.27.cloned.1.call-done = f32[16,2048]{1,0:T(8,128)} async-done(((f32[512,2048]{1,0:T(8,128)}), f32[16,2048]{1,0:T(8,128)}) %reduce-scatter.27.cloned.1.call-update) | async-done | bytes 131088 | tf_op jit(solution)/shard_map/reduce_scatter | solution.py:236
  2083.9 148.6 %reduce-scatter.17.cloned.1.call-done = f32[16,2048]{1,0:T(8,128)} async-done(((f32[512,2048]{1,0:T(8,128)}), f32[16,2048]{1,0:T(8,128)}) %reduce-scatter.17.cloned.1.call-update) | async-done | bytes 131088 | tf_op jit(solution)/shard_map/reduce_scatter | solution.py:236
  2232.5 150.0 %reduce-scatter.19.cloned.1.call-done = f32[64,512]{1,0:T(8,128)} async-done(((f32[2048,512]{1,0:T(8,128)}), f32[64,512]{1,0:T(8,128)}) %reduce-scatter.19.cloned.1.call-update) | async-done | bytes 131088 | tf_op jit(solution)/shard_map/reduce_scatter | solution.py:237
  (686 shorter events, 404.5 us)
Async XLA Ops:
  7.2 91.3 %copy-start.163 = (bf16[5,16]{1,0:T(8,128)(2,1)S(1)}, bf16[5,16]{1,0:T(8,128)(2,1)}, u32[]{:S(2)}) copy-start(bf16[5,16]{1,0:T(8,128)(2,1)} %param.43) | copy-start | bytes 484
  7.2 156.5 %copy-start.164 = (bf16[5,16]{1,0:T(8,128)(2,1)S(1)}, bf16[5,16]{1,0:T(8,128)(2,1)}, u32[]{:S(2)}) copy-start(bf16[5,16]{1,0:T(8,128)(2,1)} %param.44) | copy-start | bytes 484
  7.2 223.7 %copy-start.135 = (bf16[16,512]{1,0:T(8,128)(2,1)S(1)}, bf16[16,512]{1,0:T(8,128)(2,1)}, u32[]{:S(2)}) copy-start(bf16[16,512]{1,0:T(8,128)(2,1)} %param.38) | copy-start | bytes 49156
  7.2 376.5 %all-gather.14.cloned.1.call-start = ((), (), s32[]{:S(2)}) async-start(), calls=%async_computation.12 | async-start | bytes 1622016 | tf_op jit(solution)/shard_map/all_gather | solution.py:264
  7.9 418.5 %all-gather.10.cloned.1.call-start = ((), (), s32[]{:S(2)}) async-start(), calls=%async_computation.10 | async-start | bytes 1622016 | tf_op jit(solution)/shard_map/all_gather | solution.py:201
  8.7 465.4 %all-gather.12.cloned.1.call-start = ((), (), s32[]{:S(2)}) async-start(), calls=%async_computation.11 | async-start | bytes 1622016 | tf_op jit(solution)/shard_map/all_gather | solution.py:201
  9.4 472.8 %all-gather.16.cloned.1.call-start = ((), (), s32[]{:S(2)}) async-start(), calls=%async_computation.13 | async-start | bytes 2162688 | tf_op jit(solution)/shard_map/all_gather | solution.py:208
  10.0 295.0 %copy-start.84 = (bf16[1,1024,512]{2,1,0:T(8,128)(2,1)S(1)}, bf16[1,1024,512]{2,1,0:T(8,128)(2,1)}, u32[]{:S(2)}) copy-start(bf16[1,1024,512]{2,1,0:T(8,128)(2,1)} %param.30) | copy-start | bytes 3145732
  10.0 480.4 %all-gather.18.cloned.1.call-start = ((), (), s32[]{:S(2)}) async-start(), calls=%async_computation.14 | async-start | bytes 2162688 | tf_op jit(solution)/shard_map/all_gather | solution.py:209
  10.6 528.6 %all-gather.20.cloned.1.call-start = ((), (), s32[]{:S(2)}) async-start(), calls=%async_computation.15 | async-start | bytes 2162688 | tf_op jit(solution)/shard_map/all_gather | solution.py:208
  11.2 536.2 %all-gather.22.cloned.1.call-start = ((), (), s32[]{:S(2)}) async-start(), calls=%async_computation.16 | async-start | bytes 2162688 | tf_op jit(solution)/shard_map/all_gather | solution.py:209
  11.9 997.0 %reduce-scatter.33.cloned.1.call-start = ((), (), s32[]{:S(2)}) async-start(), calls=%async_computation.26 | async-start | bytes 270336
  98.4 207.9 %copy-start.136 = (bf16[16,512]{1,0:T(8,128)(2,1)S(1)}, bf16[16,512]{1,0:T(8,128)(2,1)}, u32[]{:S(2)}) copy-start(bf16[16,512]{1,0:T(8,128)(2,1)} %param.40) | copy-start | bytes 49156
  98.4 283.9 %copy-start.83 = (bf16[1,1024,512]{2,1,0:T(8,128)(2,1)S(1)}, bf16[1,1024,512]{2,1,0:T(8,128)(2,1)}, u32[]{:S(2)}) copy-start(bf16[1,1024,512]{2,1,0:T(8,128)(2,1)} %param.45) | copy-start | bytes 3145732
  306.3 77.4 %copy-start.88 = (bf16[1,1024,512]{2,1,0:T(8,128)(2,1)S(1)}, bf16[1,1024,512]{2,1,0:T(8,128)(2,1)}, u32[]{:S(2)}) copy-start(bf16[1,1024,512]{2,1,0:T(8,128)(2,1)} %param.29) | copy-start | bytes 3145732
  424.9 65.5 %copy-start.115 = (f32[1024]{0:T(1024)}, f32[1024]{0:T(1024)S(1)}, u32[]{:S(2)}) copy-start(f32[1024]{0:T(1024)S(1)} %broadcast_multiply_fusion.13) | copy-start | bytes 12292
  426.5 64.0 %copy-start.137 = (f32[1024]{0:T(1024)}, f32[1024]{0:T(1024)S(1)}, u32[]{:S(2)}) copy-start(f32[1024]{0:T(1024)S(1)} %add_rsqrt_fusion.3) | copy-start | bytes 12292
  473.8 62.7 %copy-start.23 = (f32[1024,512]{0,1:T(8,128)}, f32[1024,512]{0,1:T(8,128)S(1)}, u32[]{:S(2)}) copy-start(f32[1024,512]{0,1:T(8,128)S(1)} %get-tuple-element.1059) | copy-start | bytes 6291460
  473.8 62.7 %copy-start.108 = (f32[1024]{0:T(1024)}, f32[1024]{0:T(1024)S(1)}, u32[]{:S(2)}) copy-start(f32[1024]{0:T(1024)S(1)} %broadcast_multiply_fusion.14) | copy-start | bytes 12292
  537.5 33.9 %copy-start.123 = (f32[1024]{0:T(1024)}, f32[1024]{0:T(1024)S(1)}, u32[]{:S(2)}) copy-start(f32[1024]{0:T(1024)S(1)} %broadcast_multiply_fusion.11) | copy-start | bytes 12292
  539.2 32.2 %copy-start.141 = (f32[1024]{0:T(1024)}, f32[1024]{0:T(1024)S(1)}, u32[]{:S(2)}) copy-start(f32[1024]{0:T(1024)S(1)} %add_rsqrt_fusion.1) | copy-start | bytes 12292
  539.2 8.2 copy-start.39
  547.4 12.2 copy-start.179
  554.9 12.4 copy-start.37
  554.9 12.3 copy-start.113
  555.2 12.0 copy-start.133
  611.8 13.0 copy-start
  652.8 13.0 copy-start
  671.4 11.5 copy-start.47
  680.4 8.0 slice-start
  682.9 13.0 copy-start.75
  701.7 353.6 %reduce-scatter.31.cloned.1.call-start = ((), (), s32[]{:S(2)}) async-start(), calls=%async_computation.25 | async-start | bytes 270336
  742.5 13.0 copy-start.1
  747.8 7.7 copy-start.16
  785.2 13.0 copy-start.1
  790.4 7.8 copy-start.16
  854.5 13.0 copy-start.2
  894.3 13.0 copy-start.2
  899.5 7.7 copy-start.17
  925.6 311.0 %all-reduce.5.cloned.1.call-start = ((), (), s32[]{:S(2)}) async-start(), calls=%async_computation.27 | async-start | bytes 16777216
  939.0 435.8 %reduce-scatter.21.cloned.1.call-start = ((), (), s32[]{:S(2)}) async-start(), calls=%async_computation.20 | async-start | bytes 1081344 | tf_op jit(solution)/shard_map/reduce_scatter | solution.py:230
  942.6 567.0 %reduce-scatter.25.cloned.1.call-start = ((), (), s32[]{:S(2)}) async-start(), calls=%async_computation.22 | async-start | bytes 1081344 | tf_op jit(solution)/shard_map/reduce_scatter | solution.py:230
  946.5 697.9 %reduce-scatter.15.cloned.1.call-start = ((), (), s32[]{:S(2)}) async-start(), calls=%async_computation.17 | async-start | bytes 1081344 | tf_op jit(solution)/shard_map/reduce_scatter | solution.py:361
  949.9 835.3 %reduce-scatter.23.cloned.1.call-start = ((), (), s32[]{:S(2)}) async-start(), calls=%async_computation.21 | async-start | bytes 3244032 | tf_op jit(solution)/shard_map/reduce_scatter | solution.py:229
  957.2 977.4 %reduce-scatter.29.cloned.1.call-start = ((), (), s32[]{:S(2)}) async-start(), calls=%async_computation.24 | async-start | bytes 4325376 | tf_op jit(solution)/shard_map/reduce_scatter | solution.py:237
  969.0 1114.9 %reduce-scatter.27.cloned.1.call-start = ((), (), s32[]{:S(2)}) async-start(), calls=%async_computation.23 | async-start | bytes 4325376 | tf_op jit(solution)/shard_map/reduce_scatter | solution.py:236
  976.9 1255.5 %reduce-scatter.17.cloned.1.call-start = ((), (), s32[]{:S(2)}) async-start(), calls=%async_computation.18 | async-start | bytes 4325376 | tf_op jit(solution)/shard_map/reduce_scatter | solution.py:236
  985.0 1397.5 %reduce-scatter.19.cloned.1.call-start = ((), (), s32[]{:S(2)}) async-start(), calls=%async_computation.19 | async-start | bytes 4325376 | tf_op jit(solution)/shard_map/reduce_scatter | solution.py:237
  (175 other events, 518.6 us)
Sparse Core Ops, SparseCore 0:
  11.0 57.9 all-gather.13
  72.0 54.4 all-gather.9
  129.5 53.9 all-gather.11
  186.3 55.6 all-gather.15
  244.7 55.8 all-gather.17
  303.4 56.1 all-gather.19
  362.5 55.3 all-gather.21
  701.8 129.4 reduce-scatter.32
  925.7 129.5 reduce-scatter.30
  1061.0 175.4 all-reduce.4
  1239.3 135.3 reduce-scatter.20
  1377.5 132.0 reduce-scatter.24
  1512.4 131.9 reduce-scatter.14
  1647.2 137.9 reduce-scatter.22
  1787.9 146.5 reduce-scatter.28
  1937.2 146.5 reduce-scatter.26
  2086.6 145.8 reduce-scatter.16
  2235.2 147.2 reduce-scatter.18
where the time goes:
time: 2400 us; the launch traced here: 2390 us
  waiting for transfers between devices  1370 us (57%)
  matrix products  375 us (16%)
  blocking collectives  360 us (15%)
  local copies, waits for them, and re-layouts  140 us (6%)
  other arithmetic  115 us (5%)
    reduce_scatter x2, waiting for transfers between devices, reduce_ffn(): lax.psum_scatter(down_grad, ('wide', 'narrow'), scatter_dimension=0, tile...  299 us
    reduce_scatter x2, waiting for transfers between devices, reduce_ffn(): lax.psum_scatter(up_grad, ('wide', 'narrow'), scatter_dimension=0, tiled=...  298 us
    reduce_scatter x2, waiting for transfers between devices, reduce_attention(): lax.psum_scatter(mix_grad, ('wide', 'narrow'), scatter_dimension=0, tiled...  270 us
    unnamed x21, waiting for transfers between devices  229 us
    all_gather x2, blocking collectives, fetch_attention(): lax.all_gather(mix_shard, ('wide', 'narrow'), axis=0, tiled=True)  150 us
    reduce_scatter x1, waiting for transfers between devices, reduce_attention(): lax.psum_scatter(proj_grad, ('wide', 'narrow'), scatter_dimension=1, tile...  141 us
    reduce_scatter x1, waiting for transfers between devices, on_device(): lax.psum_scatter(mix_grad, ('wide', 'narrow'), scatter_dimension=0, tiled...  135 us
    dot_general x12, matrix products, block_scores(): jnp.einsum('qhd,khd->hqk', query_block, key_row, preferred_element_type=j...  89.3 us
  transfers between devices with their start and end apart: 18, of which 10 were waited for; matrix products, arithmetic and copies ran while one was open for 18% of the time, Pallas kernels for 0%

commit v1 on v0

--- a/solution.py
+++ b/solution.py
@@ -196,46 +196,46 @@
     return (project_back(grad_hidden, up_weight), up_grad, down_grad)
 
 
-def fetch_attention(proj_shard, mix_shard):
-    return (
-        lax.all_gather(proj_shard, ("wide", "narrow"), axis=1, tiled=True),
-        lax.all_gather(mix_shard, ("wide", "narrow"), axis=0, tiled=True),
-    )
-
-
-def fetch_ffn(up_shard, down_shard):
-    return (
-        lax.all_gather(up_shard, ("wide", "narrow"), axis=0, tiled=True),
-        lax.all_gather(down_shard, ("wide", "narrow"), axis=0, tiled=True),
-    )
-
-
-def attention_again(proj_shard, mix_shard):
-    return (
-        lax.all_gather(proj_shard, ("wide", "narrow"), axis=1, tiled=True),
-        lax.all_gather(mix_shard, ("wide", "narrow"), axis=0, tiled=True),
-    )
-
-
-def ffn_again(up_shard, down_shard):
-    return (
-        lax.all_gather(up_shard, ("wide", "narrow"), axis=0, tiled=True),
-        lax.all_gather(down_shard, ("wide", "narrow"), axis=0, tiled=True),
-    )
-
-
-def reduce_attention(proj_grad, mix_grad):
-    return (
-        lax.psum_scatter(proj_grad, ("wide", "narrow"), scatter_dimension=1, tiled=True),
-        lax.psum_scatter(mix_grad, ("wide", "narrow"), scatter_dimension=0, tiled=True),
-    )
-
-
-def reduce_ffn(up_grad, down_grad):
-    return (
-        lax.psum_scatter(up_grad, ("wide", "narrow"), scatter_dimension=0, tiled=True),
-        lax.psum_scatter(down_grad, ("wide", "narrow"), scatter_dimension=0, tiled=True),
-    )
+def gather_all(shards):
+    count = lax.axis_size(("wide", "narrow"))
+    flat = [jnp.reshape(item, (-1, 512)) for item in shards]
+    whole = lax.all_gather(jnp.concatenate(flat), ("wide", "narrow"), axis=0, tiled=False)
+    whole = whole.reshape(count, -1, 512)
+    parts = []
+    start = 0
+    for item, piece in zip(shards, flat):
+        stop = start + piece.shape[0]
+        block = whole[:, start:stop]
+        start = stop
+        if item.ndim == 3:
+            block = block.reshape(count, item.shape[0], -1, item.shape[2])
+            block = jnp.moveaxis(block, 0, 1)
+            parts.append(block.reshape(item.shape[0], -1, item.shape[2]))
+        else:
+            parts.append(block.reshape(-1, item.shape[1]))
+    return parts
+
+
+def scatter_all(grads, shards):
+    count = lax.axis_size(("wide", "narrow"))
+    flat = []
+    for grad in grads:
+        if grad.ndim == 3:
+            block = grad.reshape(grad.shape[0], count, -1, grad.shape[2])
+            block = jnp.moveaxis(block, 1, 0)
+        else:
+            block = grad
+        flat.append(block.astype(jnp.bfloat16).reshape(count, -1, 512))
+    whole = jnp.concatenate(flat, axis=1)
+    whole = lax.psum_scatter(whole, "wide", scatter_dimension=0, tiled=True)
+    whole = lax.psum_scatter(whole, "narrow", scatter_dimension=0, tiled=True)[0]
+    parts = []
+    start = 0
+    for item in shards:
+        stop = start + item.size // 512
+        parts.append(whole[start:stop].astype(jnp.float32).reshape(item.shape))
+        start = stop
+    return parts
 
 
 def on_device(
@@ -260,12 +260,14 @@
     width = source.shape[-1]
     source_low = source.reshape(-1, width)
     target_low = target.reshape(-1, width)
-    enc_proj_all, enc_mix_all, gain_all, bias_all = (
-        lax.all_gather(encoder_proj, ("wide", "narrow"), axis=1, tiled=True),
-        lax.all_gather(encoder_mix, ("wide", "narrow"), axis=0, tiled=True),
-        lax.all_gather(norm_gain, ("wide", "narrow"), axis=1, tiled=True),
-        lax.all_gather(norm_bias, ("wide", "narrow"), axis=1, tiled=True),
-    )
+    shards = (encoder_proj, encoder_mix, encoder_up, encoder_down, self_proj, self_mix)
+    shards += (cross_proj, cross_mix, decoder_up, decoder_down)
+    weights = gather_all(shards)
+    enc_proj_all, enc_mix_all = weights[:2]
+    norm_all = lax.all_gather(
+        jnp.concatenate([norm_gain, norm_bias]), ("wide", "narrow"), axis=1, tiled=True
+    )
+    gain_all, bias_all = norm_all[:5], norm_all[5:]
     gains = gain_all.astype(jnp.float32)
     biases = bias_all.astype(jnp.float32)
     branch, enc_attn_saved = attention_forward(
@@ -273,37 +275,37 @@
     )
     first, norm_first = layer_norm(source_low.astype(jnp.float32) + branch, gains[0], biases[0])
     first_low = first.astype(jnp.bfloat16)
-    enc_ffn_all = fetch_ffn(encoder_up, encoder_down)
+    enc_ffn_all = weights[2:4]
     branch, enc_ffn_saved = ffn_forward(first_low, enc_ffn_all[0], enc_ffn_all[1])
     encoded, norm_encoded = layer_norm(first + branch, gains[1], biases[1])
     encoded_low = encoded.astype(jnp.bfloat16)
-    self_all = fetch_attention(self_proj, self_mix)
+    self_all = weights[4:6]
     branch, self_saved = attention_forward(
         target_low, target_low, self_all[0], self_all[1], target_segments, target_segments, True
     )
     second, norm_second = layer_norm(target_low.astype(jnp.float32) + branch, gains[2], biases[2])
     second_low = second.astype(jnp.bfloat16)
-    cross_all = fetch_attention(cross_proj, cross_mix)
+    cross_all = weights[6:8]
     branch, cross_saved = attention_forward(
         second_low, encoded_low, cross_all[0], cross_all[1], target_segments, source_segments, False
     )
     third, norm_third = layer_norm(second + branch, gains[3], biases[3])
     third_low = third.astype(jnp.bfloat16)
-    dec_ffn_all = fetch_ffn(decoder_up, decoder_down)
+    dec_ffn_all = weights[8:10]
     branch, dec_ffn_saved = ffn_forward(third_low, dec_ffn_all[0], dec_ffn_all[1])
     final, norm_final = layer_norm(third + branch, gains[4], biases[4])
     valid = (target_segments >= 0).reshape(-1, 1).astype(jnp.float32)
     grad_final = cotangent.reshape(-1, width).astype(jnp.float32) * valid
     grad_resid, gain_four, bias_four = layer_norm_back(grad_final, norm_final, gains[4])
-    dec_ffn_back = ffn_again(decoder_up, decoder_down)
+    dec_ffn_back = weights[8:10]
     grad_input, up_grad, down_grad = ffn_backward(
         grad_resid, third_low, dec_ffn_back[0], dec_ffn_back[1], dec_ffn_saved
     )
-    dec_up_grad, dec_down_grad = reduce_ffn(up_grad, down_grad)
+    dec_ffn_grads = [up_grad, down_grad]
     grad_resid, gain_three, bias_three = layer_norm_back(
         grad_resid + grad_input, norm_third, gains[3]
     )
-    cross_back = attention_again(cross_proj, cross_mix)
+    cross_back = weights[6:8]
     query_side, source_side, proj_grad, mix_grad = attention_backward(
         grad_resid,
         second_low,
@@ -315,10 +317,10 @@
         source_segments,
         False,
     )
-    cross_proj_grad, cross_mix_grad = reduce_attention(proj_grad, mix_grad)
+    cross_grads = [proj_grad, mix_grad]
     grad_encoded = source_side
     grad_resid, gain_two, bias_two = layer_norm_back(grad_resid + query_side, norm_second, gains[2])
-    self_back = attention_again(self_proj, self_mix)
+    self_back = weights[4:6]
     query_side, source_side, proj_grad, mix_grad = attention_backward(
         grad_resid,
         target_low,
@@ -330,18 +332,18 @@
         target_segments,
         True,
     )
-    self_proj_grad, self_mix_grad = reduce_attention(proj_grad, mix_grad)
+    self_grads = [proj_grad, mix_grad]
     target_grad = grad_resid + query_side + source_side
     grad_resid, gain_one, bias_one = layer_norm_back(grad_encoded, norm_encoded, gains[1])
-    enc_ffn_back = ffn_again(encoder_up, encoder_down)
+    enc_ffn_back = weights[2:4]
     grad_input, up_grad, down_grad = ffn_backward(
         grad_resid, first_low, enc_ffn_back[0], enc_ffn_back[1], enc_ffn_saved
     )
-    enc_up_grad, enc_down_grad = reduce_ffn(up_grad, down_grad)
+    enc_ffn_grads = [up_grad, down_grad]
     grad_resid, gain_zero, bias_zero = layer_norm_back(
         grad_resid + grad_input, norm_first, gains[0]
     )
-    enc_back = attention_again(encoder_proj, encoder_mix)
+    enc_back = weights[0:2]
     query_side, source_side, proj_grad, mix_grad = attention_backward(
         grad_resid,
         source_low,
@@ -356,12 +358,23 @@
     source_grad = grad_resid + query_side + source_side
     gain_grad = jnp.stack([gain_zero, gain_one, gain_two, gain_three, gain_four])
     bias_grad = jnp.stack([bias_zero, bias_one, bias_two, bias_three, bias_four])
-    enc_proj_grad, enc_mix_grad, gain_shard, bias_shard = (
-        lax.psum_scatter(proj_grad, ("wide", "narrow"), scatter_dimension=1, tiled=True),
-        lax.psum_scatter(mix_grad, ("wide", "narrow"), scatter_dimension=0, tiled=True),
-        lax.psum_scatter(gain_grad, ("wide", "narrow"), scatter_dimension=1, tiled=True),
-        lax.psum_scatter(bias_grad, ("wide", "narrow"), scatter_dimension=1, tiled=True),
-    )
+    norm_grad = lax.psum_scatter(
+        jnp.concatenate([gain_grad, bias_grad]), ("wide", "narrow"), scatter_dimension=1, tiled=True
+    )
+    gain_shard, bias_shard = norm_grad[:5], norm_grad[5:]
+    grads = [proj_grad, mix_grad] + enc_ffn_grads + self_grads + cross_grads + dec_ffn_grads
+    (
+        enc_proj_grad,
+        enc_mix_grad,
+        enc_up_grad,
+        enc_down_grad,
+        self_proj_grad,
+        self_mix_grad,
+        cross_proj_grad,
+        cross_mix_grad,
+        dec_up_grad,
+        dec_down_grad,
+    ) = scatter_all(grads, shards)
     return (
         final.reshape(target.shape).astype(jnp.bfloat16),
         source_grad.reshape(source.shape).astype(jnp.bfloat16),

time: 2400 us -> 1020 us (0.42)
  waiting for transfers between devices: 1370 us -> 286 us
  blocking collectives: 360 us -> 72.8 us
  local copies, waits for them, and re-layouts: 140 us -> 184 us
  matrix products: 375 us -> 339 us
    reduce_scatter x8 -> x2, waiting for transfers between devices: 1140 us -> 137 us  [the longest x1 100 us: scatter_all(): whole = lax.psum_scatter(whole, 'wide', scatter_dimension=0, tiled=True)]
    all_gather x5 -> x1, blocking collectives: 360 us -> 72.8 us  [on_device(): lax.all_gather(jnp.concatenate([norm_gain, norm_bias]), ('wide', 'narrow'...]
    unnamed x21 -> x5, waiting for transfers between devices: 229 us -> 123 us
    all_gather x7 -> x1, waiting for transfers between devices: 0.07 us -> 26.7 us  [gather_all(): lax.all_gather(jnp.concatenate(flat), ('wide', 'narrow'), axis=0, tiled=F...]
    unnamed x347 -> x334, local copies, waits for them, and re-layouts: 43.2 us -> 51.7 us
  transfers between devices with their start and end apart: 18 -> 4, of which waited for: 10 -> 4; matrix products, arithmetic and copies ran while one was open for 18% -> 2% of each run, Pallas kernels for 0% -> 0%
where the time goes in v1:
time: 1020 us
  matrix products  339 us (33%)
  waiting for transfers between devices  286 us (28%)
  local copies, waits for them, and re-layouts  184 us (18%)
  other arithmetic  109 us (11%)
  blocking collectives  72.8 us (7%)
  between operations  15.9 us (2%)
  loops' own time  10.3 us (1%)
    unnamed x5, waiting for transfers between devices  123 us
    reduce_scatter x1, waiting for transfers between devices, scatter_all(): whole = lax.psum_scatter(whole, 'wide', scatter_dimension=0, tiled=True)  100 us
    dot_general x12, matrix products, block_scores(): jnp.einsum('qhd,khd->hqk', query_block, key_row, preferred_element_type=j...  91.6 us
    all_gather x1, blocking collectives, on_device(): lax.all_gather(jnp.concatenate([norm_gain, norm_bias]), ('wide', 'narrow'...  72.8 us
    unnamed x334, local copies, waits for them, and re-layouts  51.7 us
    dot_general x6, matrix products, one_block(): jnp.einsum('hqk,khd->qhd', grad_scores, key_row, preferred_element_type=j...  46.2 us
    dot_general x16, matrix products, project_back(): jnp.einsum('nf,df->nd', grad, weight, preferred_element_type=jnp.float32)  44.5 us
    convert_element_type x6, other arithmetic, one_block(): grad_scores = (probs * (grad_probs - inner)).astype(jnp.bfloat16)  41.3 us
  transfers between devices with their start and end apart: 4, of which 4 were waited for; matrix products, arithmetic and copies ran while one was open for 2% of the time, Pallas kernels for 0%

profile of v1, /device:TPU:0, one launch (start us, length us, event | category | flops | bytes accessed | tf_op | source)
XLA Modules:
  0.0 1016.7 jit_solution(12888711374075621486)
XLA Ops:
  23.1 72.8 %all_gather.11 = bf16[10,512]{0,1:T(8,128)(2,1)S(1)} all-gather(bf16[10,16]{0,1:T(8,128)(2,1)S(1)} %pad_maximum_fusion), channel_id=1, replica_groups=mesh['wide'=8,'narrow'=4] {'wide','narrow'}, dimensions={1}, use_global_device_ids=true | all-gather | bytes 10560 | tf_op jit(solution)/shard_map/all_gather | solution.py:267
  98.6 26.7 %all-gather.3.cloned.1.call-done = bf16[14336,512]{1,0:T(8,128)(2,1)} async-done(((bf16[448,512]{1,0:T(8,128)(2,1)}), bf16[14336,512]{1,0:T(8,128)(2,1)}) %all-gather.3.cloned.1.call-update) | async-done | bytes 14680080 | tf_op jit(solution)/shard_map/all_gather | solution.py:202
  125.3 4.3 fusion.189
  132.2 6.5 fusion.187
  147.9 27.1 %while.87 = (s32[]{:T(128)}, bf16[2,512,8,64]{1,3,2,0:T(8,128)(2,1)}, f32[2,8,512]{2,1,0:T(8,128)S(1)}, s32[2,512]{1,0:T(2,128)S(1)}, s32[1,1024]{1,0:T(1,128)S(...) while((s32[]{:T(128)}, ...), condition=%wide.region_9.10_spmd, body=%wide.region_6.9_spmd.sunk | while | flops 1120661504 | bytes 64104612 | solution.py:93
  155.5 4.9 fusion.323
  169.1 4.9 fusion.323
  179.8 4.9 reshape.892
  184.8 4.3 fusion.183
  208.1 35.0 %while.86 = (s32[]{:T(128)}, bf16[2,512,8,64]{1,3,2,0:T(8,128)(2,1)}, f32[2,8,512]{2,1,0:T(8,128)S(1)}, s32[2,512]{1,0:T(2,128)S(1)}, s32[1,1024]{1,0:T(1,128)S(...) while((s32[]{:T(128)}, ...), condition=%wide.region_3.4_spmd, body=%wide.region_0.3_spmd.sunk | while | flops 1121710592 | bytes 64109384 | solution.py:93
  219.8 4.9 fusion.320
  237.2 4.9 fusion.320
  259.5 30.7 %while.88 = (s32[]{:T(128)}, bf16[2,512,8,64]{1,3,2,0:T(8,128)(2,1)}, f32[2,8,512]{2,1,0:T(8,128)S(1)}, s32[2,512]{1,0:T(2,128)S(1)}, s32[1,1024]{1,0:T(1,128)S(...) while((s32[]{:T(128)}, ...), condition=%wide.region_17.18_spmd, body=%wide.region_14.17_spmd.sunk | while | flops 1120661504 | bytes 64105120 | solution.py:93
  268.7 5.4 fusion.326
  283.9 5.4 fusion.326
  295.5 4.6 reshape.898
  312.1 7.8 fusion.126
  319.8 5.8 convolution_convert_fusion
  349.0 82.5 %while.89 = (s32[]{:T(128)}, bf16[2,512,8,64]{1,3,2,0:T(8,128)(2,1)}, f32[2,1024,8,64]{1,3,2,0:T(8,128)}, f32[2,1024,8,64]{1,3,2,0:T(8,128)}, s32[2,512]{1,0:T(2...) while((s32[]{:T(128)}, ...), condition=%wide.region_28.29_spmd, body=%wide.region_26.28_spmd.sunk | while | flops 2723672064 | bytes 242054928 | solution.py:140
  355.9 11.5 %multiply_reduce_fusion.23 = (f32[8,512]{1,0:T(8,128)}, f32[8,512,1024]{2,1,0:T(8,128)}) fusion(f32[8,512,1024]{2,1,0:T(8,128)S(1)} %fusion.335, f32[8,512]{1,0:T(8,128)} %dynamic-slice_bitcast_fusion.6, bf16[1,1024,8,64]{1,3,2,0:T(8,128)(2,1)S(1)} %get-tuple-element.1628, bf16[2,512,8,64]{1,3,2,0:T(8,128)(2,1)} %get-tuple-element.1627, ...), kind=kOutput, calls=%fused_computation.66.clone.1 | convolution fusion | flops 557838336 | bytes 35684864 | tf_op jit(solution)/shard_map/while/body/eval_jaxpr/qhd,khd->hqk/dot_general | solution.py:55
  367.4 6.8 multiply_convert_fusion.12
  374.3 4.5 bitcast_dynamic-update-slice_fusion.21
  379.5 7.7 fusion.336
  397.0 11.5 %multiply_reduce_fusion.23 = (f32[8,512]{1,0:T(8,128)}, f32[8,512,1024]{2,1,0:T(8,128)}) fusion(f32[8,512,1024]{2,1,0:T(8,128)S(1)} %fusion.335, f32[8,512]{1,0:T(8,128)} %dynamic-slice_bitcast_fusion.6, bf16[1,1024,8,64]{1,3,2,0:T(8,128)(2,1)S(1)} %get-tuple-element.1628, bf16[2,512,8,64]{1,3,2,0:T(8,128)(2,1)} %get-tuple-element.1627, ...), kind=kOutput, calls=%fused_computation.66.clone.1 | convolution fusion | flops 557838336 | bytes 35684864 | tf_op jit(solution)/shard_map/while/body/eval_jaxpr/qhd,khd->hqk/dot_general | solution.py:55
  408.5 6.8 multiply_convert_fusion.12
  415.4 4.5 bitcast_dynamic-update-slice_fusion.21
  420.6 7.7 fusion.336
  444.9 10.1 fusion.119
  467.3 4.8 convolution_convert_fusion.2
  482.6 4.5 reshape.916
  502.1 85.9 %while.91 = (s32[]{:T(128)}, bf16[2,512,8,64]{1,3,2,0:T(8,128)(2,1)}, f32[2,1024,8,64]{1,3,2,0:T(8,128)}, f32[2,1024,8,64]{1,3,2,0:T(8,128)}, s32[2,512]{1,0:T(2...) while((s32[]{:T(128)}, ...), condition=%wide.region_44.45_spmd, body=%wide.region_42.44_spmd.sunk | while | flops 2724721152 | bytes 246122544 | solution.py:140
  510.9 11.5 %multiply_reduce_fusion.25 = (f32[8,512]{1,0:T(8,128)}, f32[8,512,1024]{2,1,0:T(8,128)}) fusion(f32[8,512,1024]{2,1,0:T(8,128)S(1)} %fusion.355, f32[8,512]{1,0:T(8,128)} %dynamic-slice_bitcast_fusion.8, bf16[1,1024,8,64]{1,3,2,0:T(8,128)(2,1)S(1)} %get-tuple-element.1709, bf16[2,512,8,64]{1,3,2,0:T(8,128)(2,1)} %get-tuple-element.1708, ...), kind=kOutput, calls=%fused_computation.126.clone.1 | convolution fusion | flops 557838336 | bytes 35684864 | tf_op jit(solution)/shard_map/while/body/eval_jaxpr/qhd,khd->hqk/dot_general | solution.py:55
  522.4 6.9 multiply_convert_fusion.14
  534.6 7.7 fusion.357
  553.5 11.5 %multiply_reduce_fusion.25 = (f32[8,512]{1,0:T(8,128)}, f32[8,512,1024]{2,1,0:T(8,128)}) fusion(f32[8,512,1024]{2,1,0:T(8,128)S(1)} %fusion.355, f32[8,512]{1,0:T(8,128)} %dynamic-slice_bitcast_fusion.8, bf16[1,1024,8,64]{1,3,2,0:T(8,128)(2,1)S(1)} %get-tuple-element.1709, bf16[2,512,8,64]{1,3,2,0:T(8,128)(2,1)} %get-tuple-element.1708, ...), kind=kOutput, calls=%fused_computation.126.clone.1 | convolution fusion | flops 557838336 | bytes 35684864 | tf_op jit(solution)/shard_map/while/body/eval_jaxpr/qhd,khd->hqk/dot_general | solution.py:55
  565.1 6.9 multiply_convert_fusion.14
  577.2 7.7 fusion.357
  603.3 4.4 reshape.908
  617.3 80.1 %while.90 = (s32[]{:T(128)}, bf16[2,512,8,64]{1,3,2,0:T(8,128)(2,1)}, f32[2,1024,8,64]{1,3,2,0:T(8,128)}, f32[2,1024,8,64]{1,3,2,0:T(8,128)}, s32[2,512]{1,0:T(2...) while((s32[]{:T(128)}, ...), condition=%wide.region_37.38_spmd, body=%wide.region_35.37_spmd.sunk | while | flops 2723672064 | bytes 246118160 | solution.py:140
  623.0 11.5 %multiply_reduce_fusion.24 = (f32[8,512]{1,0:T(8,128)}, f32[8,512,1024]{2,1,0:T(8,128)}) fusion(f32[8,512,1024]{2,1,0:T(8,128)S(1)} %fusion.345, f32[8,512]{1,0:T(8,128)} %dynamic-slice_bitcast_fusion.7, bf16[1,1024,8,64]{1,3,2,0:T(8,128)(2,1)S(1)} %get-tuple-element.1664, bf16[2,512,8,64]{1,3,2,0:T(8,128)(2,1)} %get-tuple-element.1663, ...), kind=kOutput, calls=%fused_computation.96.clone.1 | convolution fusion | flops 557838336 | bytes 35684864 | tf_op jit(solution)/shard_map/while/body/eval_jaxpr/qhd,khd->hqk/dot_general | solution.py:55
  634.5 6.9 multiply_convert_fusion.13
  646.7 7.7 fusion.346
  662.9 11.5 %multiply_reduce_fusion.24 = (f32[8,512]{1,0:T(8,128)}, f32[8,512,1024]{2,1,0:T(8,128)}) fusion(f32[8,512,1024]{2,1,0:T(8,128)S(1)} %fusion.345, f32[8,512]{1,0:T(8,128)} %dynamic-slice_bitcast_fusion.7, bf16[1,1024,8,64]{1,3,2,0:T(8,128)(2,1)S(1)} %get-tuple-element.1664, bf16[2,512,8,64]{1,3,2,0:T(8,128)(2,1)} %get-tuple-element.1663, ...), kind=kOutput, calls=%fused_computation.96.clone.1 | convolution fusion | flops 557838336 | bytes 35684864 | tf_op jit(solution)/shard_map/while/body/eval_jaxpr/qhd,khd->hqk/dot_general | solution.py:55
  674.4 6.9 multiply_convert_fusion.13
  686.6 7.7 fusion.346
  728.2 100.3 %reduce-scatter.6.cloned.1.call-done = bf16[4,448,512]{2,1,0:T(8,128)(2,1)} async-done(((bf16[32,448,512]{2,1,0:T(8,128)(2,1)}), bf16[4,448,512]{2,1,0:T(8,128)(2,1)}) %reduce-scatter.6.cloned.1.call-update) | async-done | bytes 1835024 | tf_op jit(solution)/shard_map/reduce_scatter | solution.py:230
  841.7 122.4 %reduce-scatter.10.cloned.1.call-done = f32[16,10]{1,0:T(8,128)} async-done(((f32[512,10]{1,0:T(8,128)}), f32[16,10]{1,0:T(8,128)}) %reduce-scatter.10.cloned.1.call-update) | async-done | bytes 656
  966.3 36.3 %reduce-scatter.8.cloned.1.call-done = bf16[1,448,512]{2,1,0:T(8,128)(2,1)} async-done(((bf16[4,448,512]{2,1,0:T(8,128)(2,1)}), bf16[1,448,512]{2,1,0:T(8,128)(2,1)}) %reduce-scatter.8.cloned.1.call-update) | async-done | bytes 458768 | tf_op jit(solution)/shard_map/reduce_scatter | solution.py:231
  (655 shorter events, 373.8 us)
Async XLA Ops:
  7.2 11.0 %copy-start.107 = (bf16[1,1024,512]{2,1,0:T(8,128)(2,1)S(1)}, bf16[1,1024,512]{2,1,0:T(8,128)(2,1)}, u32[]{:S(2)}) copy-start(bf16[1,1024,512]{2,1,0:T(8,128)(2,1)} %param.29) | copy-start | bytes 3145732
  7.2 12.3 %copy-start.161 = (bf16[5,16]{1,0:T(8,128)(2,1)S(1)}, bf16[5,16]{1,0:T(8,128)(2,1)}, u32[]{:S(2)}) copy-start(bf16[5,16]{1,0:T(8,128)(2,1)} %param.43) | copy-start | bytes 484
  7.2 12.4 %copy-start.162 = (bf16[5,16]{1,0:T(8,128)(2,1)S(1)}, bf16[5,16]{1,0:T(8,128)(2,1)}, u32[]{:S(2)}) copy-start(bf16[5,16]{1,0:T(8,128)(2,1)} %param.44) | copy-start | bytes 484
  7.2 12.5 %copy-start.114 = (s32[1,1024]{1,0:T(1,128)S(1)}, s32[1,1024]{1,0:T(1,128)}, u32[]{:S(2)}) copy-start(s32[1,1024]{1,0:T(1,128)} %param.32) | copy-start | bytes 12292
  7.2 13.2 %copy-start.103 = (bf16[1,1024,512]{2,1,0:T(8,128)(2,1)S(1)}, bf16[1,1024,512]{2,1,0:T(8,128)(2,1)}, u32[]{:S(2)}) copy-start(bf16[1,1024,512]{2,1,0:T(8,128)(2,1)} %param.30) | copy-start | bytes 3145732
  7.2 118.1 %all-gather.3.cloned.1.call-start = ((), (), s32[]{:S(2)}) async-start(), calls=%async_computation.5 | async-start | bytes 15138816 | tf_op jit(solution)/shard_map/all_gather | solution.py:202
  16.3 812.2 %reduce-scatter.6.cloned.1.call-start = ((), (), s32[]{:S(2)}) async-start(), calls=%async_computation.3 | async-start | bytes 16515072 | tf_op jit(solution)/shard_map/reduce_scatter | solution.py:230
  98.0 91.1 %copy-start.150 = (f32[512]{0:T(512)}, f32[512]{0:T(512)S(1)}, u32[]{:S(2)}) copy-start(f32[512]{0:T(512)S(1)} %get-tuple-element.1104) | copy-start | bytes 6148
  98.0 91.1 %copy-start.158 = (f32[512]{0:T(512)}, f32[512]{0:T(512)S(1)}, u32[]{:S(2)}) copy-start(f32[512]{0:T(512)S(1)} %get-tuple-element.917) | copy-start | bytes 6148
  98.0 97.9 %copy-start.141 = (f32[512]{0:T(512)}, f32[512]{0:T(512)S(1)}, u32[]{:S(2)}) copy-start(f32[512]{0:T(512)S(1)} %get-tuple-element.1105) | copy-start | bytes 6148
  179.5 9.6 copy-start.28
  179.5 9.6 copy-start.137
  179.8 9.3 copy-start.144
  247.5 45.3 %copy-start.15 = (f32[1024,512]{0,1:T(8,128)}, f32[1024,512]{0,1:T(8,128)S(1)}, u32[]{:S(2)}) copy-start(f32[1024,512]{0,1:T(8,128)S(1)} %get-tuple-element.1090) | copy-start | bytes 6291460
  247.5 45.3 %copy-start.131 = (f32[1024]{0:T(1024)}, f32[1024]{0:T(1024)S(1)}, u32[]{:S(2)}) copy-start(f32[1024]{0:T(1024)S(1)} %broadcast_multiply_fusion.14) | copy-start | bytes 12292
  247.8 45.0 %copy-start.135 = (f32[1024]{0:T(1024)}, f32[1024]{0:T(1024)S(1)}, u32[]{:S(2)}) copy-start(f32[1024]{0:T(1024)S(1)} %add_rsqrt_fusion.4) | copy-start | bytes 12292
  319.8 5.8 copy-start.78
  374.2 5.3 copy-start.3
  374.2 13.0 %copy-start = (f32[8,512,1024]{2,1,0:T(8,128)S(1)}, f32[8,512,1024]{2,1,0:T(8,128)}, u32[]{:S(2)}) copy-start(f32[8,512,1024]{2,1,0:T(8,128)} %get-tuple-element.1475) | copy-start | bytes 50331652 | tf_op jit(solution)/shard_map/while
  379.5 7.7 copy-start.19
  415.4 13.0 %copy-start = (f32[8,512,1024]{2,1,0:T(8,128)S(1)}, f32[8,512,1024]{2,1,0:T(8,128)}, u32[]{:S(2)}) copy-start(f32[8,512,1024]{2,1,0:T(8,128)} %get-tuple-element.1475) | copy-start | bytes 50331652 | tf_op jit(solution)/shard_map/while
  420.6 7.7 copy-start.19
  444.9 10.1 copy-start.29
  444.9 10.1 copy-start.76
  444.9 10.1 copy-start.138
  444.9 10.1 copy-start.145
  444.9 10.1 copy-start.151
  455.1 12.2 %slice-start = ((s8[8388608]{0:T(1024)(128)(4,1)}), s8[4194304]{0:T(1024)(128)(4,1)S(1)}, s32[]{:S(2)}) async-start(s8[8388608]{0:T(1024)(128)(4,1)} %bitcast.759), calls=%async_computation.7 | async-start | bytes 8388608
  458.8 8.5 slice-start.1
  467.3 6.3 copy-start.90
  467.3 6.3 copy-start.136
  467.3 6.3 copy-start.140
  522.4 6.9 copy-start.14
  529.4 5.3 copy-start.4
  529.4 12.9 %copy-start.1 = (f32[8,512,1024]{2,1,0:T(8,128)S(1)}, f32[8,512,1024]{2,1,0:T(8,128)}, u32[]{:S(2)}) copy-start(f32[8,512,1024]{2,1,0:T(8,128)} %get-tuple-element.1502) | copy-start | bytes 50331652 | tf_op jit(solution)/shard_map/while
  534.6 7.7 copy-start.17
  565.0 6.9 copy-start.14
  572.0 13.0 %copy-start.1 = (f32[8,512,1024]{2,1,0:T(8,128)S(1)}, f32[8,512,1024]{2,1,0:T(8,128)}, u32[]{:S(2)}) copy-start(f32[8,512,1024]{2,1,0:T(8,128)} %get-tuple-element.1502) | copy-start | bytes 50331652 | tf_op jit(solution)/shard_map/while
  577.2 7.7 copy-start.17
  634.5 6.9 copy-start.13
  641.5 12.9 %copy-start.2 = (f32[8,512,1024]{2,1,0:T(8,128)S(1)}, f32[8,512,1024]{2,1,0:T(8,128)}, u32[]{:S(2)}) copy-start(f32[8,512,1024]{2,1,0:T(8,128)} %get-tuple-element.1488) | copy-start | bytes 50331652 | tf_op jit(solution)/shard_map/while
  646.7 7.7 copy-start.18
  674.4 6.9 copy-start.13
  681.3 13.0 %copy-start.2 = (f32[8,512,1024]{2,1,0:T(8,128)S(1)}, f32[8,512,1024]{2,1,0:T(8,128)}, u32[]{:S(2)}) copy-start(f32[8,512,1024]{2,1,0:T(8,128)} %get-tuple-element.1488) | copy-start | bytes 50331652 | tf_op jit(solution)/shard_map/while
  686.6 7.7 copy-start.18
  726.5 102.0 %copy-start.52 = (bf16[64,8,2,512]{3,1,2,0:T(8,128)(2,1)S(1)}, bf16[64,8,2,512]{3,1,2,0:T(8,128)(2,1)}, u32[]{:S(2)}) copy-start(bf16[64,8,2,512]{3,1,2,0:T(8,128)(2,1)} %copy-done.51) | copy-start | bytes 3145732
  726.5 237.7 %reduce-scatter.10.cloned.1.call-start = ((), (), s32[]{:S(2)}) async-start(), calls=%async_computation.6 | async-start | bytes 270336
  728.1 274.5 %reduce-scatter.8.cloned.1.call-start = ((), (), s32[]{:S(2)}) async-start(), calls=%async_computation.4 | async-start | bytes 2293760 | tf_op jit(solution)/shard_map/reduce_scatter | solution.py:231
  (151 other events, 374.8 us)
Sparse Core Ops, SparseCore 0:
  16.4 108.9 all-gather.2
  726.6 101.8 reduce-scatter.5
  830.7 133.3 reduce-scatter.9
  966.4 36.1 reduce-scatter.7

commit v2 on v1

v2 whole, which is shorter than its diff:
```python
from functools import partial

import jax
import jax.numpy as jnp
from jax import lax
from jax.experimental import pallas as pl
from jax.experimental.pallas import tpu as pltpu
from jax.sharding import PartitionSpec as P

HEADS = 8
norm_eps = 1e-05
masked_score = -1e30
lowest = -3e38
log2_e = 1.4426950408889634
BLOCK = 128
TILE = 256
PAIR = 2
f32 = jnp.float32
bf16 = jnp.bfloat16


def dot(left, right, left_dim=1, right_dim=0):
    dims = (((left_dim,), (right_dim,)), ((), ()))
    return lax.dot_general(left, right, dims, preferred_element_type=f32)


def normalise(resid):
    mean = jnp.mean(resid, axis=-1, keepdims=True)
    centred = resid - mean
    scale_inv = lax.rsqrt(jnp.mean(centred * centred, axis=-1, keepdims=True) + norm_eps)
    return centred * scale_inv, scale_inv


def norm_back(grad, normed, scale_inv, gain):
    scaled = grad * gain
    mean_plain = jnp.mean(scaled, axis=-1, keepdims=True)
    mean_normed = jnp.mean(scaled * normed, axis=-1, keepdims=True)
    return scale_inv * (scaled - mean_plain - normed * mean_normed)


def key_ranges(query_segments, key_segments, causal):
    big = jnp.int32(1 << 30)
    query_order = jnp.where(query_segments < 0, big, query_segments).reshape(-1, BLOCK)
    key_order = jnp.where(key_segments < 0, big, key_segments).reshape(1, -1)
    first = jnp.sum((key_order < query_order[:, :1]).astype(jnp.int32), axis=1)
    stop = jnp.sum((key_order <= query_order[:, -1:]).astype(jnp.int32), axis=1)
    real = jnp.sum((key_order < big).astype(jnp.int32))
    if causal:
        stop = jnp.minimum(stop, (jnp.arange(stop.shape[0]) + 1) * BLOCK)
    start = first // 16 * 16
    tiles = (stop - start + TILE - 1) // TILE
    real_tiles = jnp.maximum((jnp.minimum(stop, real) - start + TILE - 1) // TILE, 0)
    real_tiles = jnp.where(first >= real, 0, real_tiles)
    return jnp.stack([start, tiles, real_tiles]).astype(jnp.int32)


def key_columns(key_segments):
    flat = jnp.pad(key_segments.reshape(-1), (0, TILE), constant_values=-2)
    return jnp.broadcast_to(flat[:, None], (flat.shape[0], 128))


def head_pair_mask():
    lane = lax.broadcasted_iota(jnp.int32, (1, 128), 1)
    return lane < 64


def stack_heads(block, even):
    zero = jnp.zeros_like(block)
    return jnp.concatenate([jnp.where(even, block, zero), jnp.where(even, zero, block)], axis=0)


def tile_bias(bias_ref, key_col_ref, query_row, key_start, query_start, causal):
    allowed = key_col_ref[pl.ds(key_start, TILE), :] == query_row
    if causal:
        key_place = key_start + lax.broadcasted_iota(jnp.int32, (TILE, BLOCK), 0)
        query_place = query_start + lax.broadcasted_iota(jnp.int32, (TILE, BLOCK), 1)
        allowed = allowed & (key_place <= query_place)
    bias_ref[...] = jnp.where(allowed, 0.0, masked_score).astype(f32)


def forward_kernel(causal, fresh, ranges, *refs):
    if fresh:
        (own, key_col, query_seg, proj, mix, norm_out,
         resid_out, low_out, q_out, k_out, v_out, o_out, lse_out,
         stacked, bias, acc, peak, total) = refs
    else:
        (own, norm_own, other, key_col, query_seg, proj, mix, norm_out,
         resid_out, low_out, q_out, k_out, v_out, o_out, lse_out,
         stacked, bias, acc, peak, total) = refs
    rows = own.shape[0]
    even = head_pair_mask()
    scale = 0.125 * log2_e

    def fill(step, carry):
        at = pl.multiple_of(step * TILE, TILE)
        block = own[pl.ds(at, TILE), :]
        if fresh:
            block_low = block
            key_block = block
        else:
            normed, _ = normalise(block)
            block_low = (normed * norm_own[0:1, :] + norm_own[1:2, :]).astype(bf16)
            low_out[pl.ds(at, TILE), :] = block_low
            key_block = other[pl.ds(at, TILE), :]
        query = dot(block_low, proj[0]).astype(bf16)
        q_out[pl.ds(at, TILE), :] = query
        for sub in range(TILE // BLOCK):
            for pair in range(4):
                part = query[sub * BLOCK : (sub + 1) * BLOCK, pair * 128 : (pair + 1) * 128]
                stacked[step * (TILE // BLOCK) + sub, pair] = stack_heads(part, even)
        k_out[pl.ds(at, TILE), :] = dot(key_block, proj[1]).astype(bf16)
        v_out[pl.ds(at, TILE), :] = dot(key_block, proj[2]).astype(bf16)
        return carry

    lax.fori_loop(0, rows // TILE, fill, 0)
    k_out[rows:, :] = jnp.zeros((TILE, k_out.shape[1]), bf16)
    v_out[rows:, :] = jnp.zeros((TILE, v_out.shape[1]), bf16)

    def one_block(index, carry):
        start = ranges[0, index]
        tiles = ranges[1, index]
        query_start = pl.multiple_of(index * BLOCK, BLOCK)
        query_row = query_seg[index]
        peak[...] = jnp.full(peak.shape, lowest, f32)
        total[...] = jnp.zeros(total.shape, f32)
        acc[...] = jnp.zeros(acc.shape, f32)

        def one_tile(tile, inner):
            at = pl.multiple_of(start + tile * TILE, 16)
            tile_bias(bias, key_col, query_row, at, query_start, causal)
            for pair in range(4):
                lanes = slice(pair * 128, (pair + 1) * 128)
                scores = dot(k_out[pl.ds(at, TILE), lanes], stacked[index, pair], 1, 1)
                blocked = bias[...]
                scores = scores * scale + jnp.concatenate([blocked, blocked], axis=1)
                before = peak[pair : pair + 1, :]
                after = jnp.maximum(before, jnp.max(scores, axis=0, keepdims=True))
                probs = jnp.exp2(scores - after)
                shrink = jnp.exp2(before - after)
                peak[pair : pair + 1, :] = after
                total[pair : pair + 1, :] = total[pair : pair + 1, :] * shrink + jnp.sum(
                    probs, axis=0, keepdims=True
                )
                mixed = dot(v_out[pl.ds(at, TILE), lanes], probs.astype(bf16), 0, 0)
                top = pair * 128
                acc[top : top + 64, :] = acc[top : top + 64, :] * shrink[:, :128] + mixed[:64, :128]
                acc[top + 64 : top + 128, :] = (
                    acc[top + 64 : top + 128, :] * shrink[:, 128:] + mixed[64:, 128:]
                )
            return inner

        lax.fori_loop(0, tiles, one_tile, 0)
        for pair in range(4):
            inverse = 1.0 / total[pair : pair + 1, :]
            top = pair * 128
            o_out[top : top + 64, pl.ds(query_start, BLOCK)] = (
                acc[top : top + 64, :] * inverse[:, :128]
            ).astype(bf16)
            o_out[top + 64 : top + 128, pl.ds(query_start, BLOCK)] = (
                acc[top + 64 : top + 128, :] * inverse[:, 128:]
            ).astype(bf16)
        lse_out[index] = peak[...] + jnp.log2(total[...])
        return carry

    lax.fori_loop(0, rows // BLOCK, one_block, 0)

    def finish(step, carry):
        at = pl.multiple_of(step * TILE, TILE)
        block = own[pl.ds(at, TILE), :]
        if fresh:
            block = block.astype(f32)
        else:
            normed, _ = normalise(block)
            block = normed * norm_own[0:1, :] + norm_own[1:2, :]
        resid = block + dot(o_out[:, pl.ds(at, TILE)], mix[...], 0, 0)
        resid_out[pl.ds(at, TILE), :] = resid
        if fresh:
            normed, _ = normalise(resid)
            low_out[pl.ds(at, TILE), :] = (normed * norm_out[0:1, :] + norm_out[1:2, :]).astype(bf16)
        return carry

    lax.fori_loop(0, rows // TILE, finish, 0)


def vmem(count):
    return [pl.BlockSpec(memory_space=pltpu.VMEM)] * count


def cost(flops, moved):
    return pl.CostEstimate(flops=int(flops), bytes_accessed=int(moved), transcendentals=0)


def attend_forward(own, norm_own, other, key_col, query_seg, ranges, weights, norm_out, causal):
    fresh = norm_own is None
    rows, width = own.shape
    blocks = rows // BLOCK
    ins = [own] if fresh else [own, norm_own, other]
    ins += [key_col, query_seg, *weights, norm_out]
    shapes = [
        jax.ShapeDtypeStruct((rows, width), f32),
        jax.ShapeDtypeStruct((rows, width), bf16),
        jax.ShapeDtypeStruct((rows, width), bf16),
        jax.ShapeDtypeStruct((rows + TILE, width), bf16),
        jax.ShapeDtypeStruct((rows + TILE, width), bf16),
        jax.ShapeDtypeStruct((width, rows), bf16),
        jax.ShapeDtypeStruct((blocks, 4, 2 * BLOCK), f32),
    ]
    return pl.pallas_call(
        partial(forward_kernel, causal, fresh),
        out_shape=shapes,
        in_specs=[pl.BlockSpec(memory_space=pltpu.SMEM)] + vmem(len(ins)),
        out_specs=vmem(len(shapes)),
        scratch_shapes=[
            pltpu.VMEM((blocks, 4, 2 * BLOCK, 128), bf16),
            pltpu.VMEM((TILE, BLOCK), f32),
            pltpu.VMEM((width, BLOCK), f32),
            pltpu.VMEM((4, 2 * BLOCK), f32),
            pltpu.VMEM((4, 2 * BLOCK), f32),
        ],
        compiler_params=pltpu.CompilerParams(vmem_limit_bytes=32 * 2**20),
        cost_estimate=cost(4e9, 12e6),
        name="attend_forward",
    )(ranges, *ins)


def backward_kernel(causal, same, ranges, *refs):
    if same:
        (grad, resid, norm, own, q_in, k_in, v_in, o_in, lse, key_col, query_seg, proj, mix,
         own_grad, weight_grad, norm_grad,
         sums, low, stacked, grad_stacked, inner_rows, bias, acc, dq, dk, dv) = refs
        other = own
        other_grad = None
    else:
        (grad, resid, norm, own, other, q_in, k_in, v_in, o_in, lse, key_col, query_seg, proj, mix,
         own_grad, other_grad, weight_grad, norm_grad,
         low, stacked, grad_stacked, inner_rows, bias, acc, dq, dk, dv) = refs
        sums = own_grad
    rows = own.shape[0]
    even = head_pair_mask()
    scale = 0.125 * log2_e
    norm_grad[...] = jnp.zeros(norm_grad.shape, f32)

    def prepare(step, carry):
        at = pl.multiple_of(step * TILE, TILE)
        block = grad[pl.ds(at, TILE), :]
        normed, scale_inv = normalise(resid[pl.ds(at, TILE), :])
        norm_grad[0:1, :] += jnp.sum(block * normed, axis=0, keepdims=True)
        norm_grad[1:2, :] += jnp.sum(block, axis=0, keepdims=True)
        block = norm_back(block, normed, scale_inv, norm[0:1, :])
        sums[pl.ds(at, TILE), :] = block
        block = block.astype(bf16)
        low[pl.ds(at, TILE), :] = block
        grad_mixed = dot(block, mix[...], 1, 1).astype(bf16)
        flipped = dot(mix[...], block, 1, 1).astype(bf16).astype(f32)
        flipped = flipped * o_in[:, pl.ds(at, TILE)].astype(f32)
        inner = [jnp.sum(flipped[head * 64 : (head + 1) * 64, :], axis=0, keepdims=True) for head in range(HEADS)]
        query = q_in[pl.ds(at, TILE), :]
        for sub in range(TILE // BLOCK):
            spot = step * (TILE // BLOCK) + sub
            span = slice(sub * BLOCK, (sub + 1) * BLOCK)
            rows_of = []
            for pair in range(4):
                lanes = slice(pair * 128, (pair + 1) * 128)
                stacked[spot, pair] = stack_heads(query[span, lanes], even)
                grad_stacked[spot, pair] = stack_heads(grad_mixed[span, lanes], even)
                rows_of.append(jnp.concatenate([inner[2 * pair][:, span], inner[2 * pair + 1][:, span]], axis=1))
            inner_rows[spot] = jnp.concatenate(rows_of, axis=0)
        return carry

    lax.fori_loop(0, rows // TILE, prepare, 0)
    weight_grad[3] = dot(o_in[...], low[...]).astype(bf16)
    dk[...] = jnp.zeros(dk.shape, f32)
    dv[...] = jnp.zeros(dv.shape, f32)

    def one_block(index, carry):
        start = ranges[0, index]
        tiles = ranges[2, index]
        query_start = pl.multiple_of(index * BLOCK, BLOCK)
        query_row = query_seg[index]
        acc[...] = jnp.zeros(acc.shape, f32)

        def one_tile(tile, inner):
            at = pl.multiple_of(start + tile * TILE, 16)
            tile_bias(bias, key_col, query_row, at, query_start, causal)
            for pair in range(4):
                lanes = slice(pair * 128, (pair + 1) * 128)
                key = k_in[pl.ds(at, TILE), lanes]
                query = stacked[index, pair]
                grad_out = grad_stacked[index, pair]
                scores = dot(key, query, 1, 1)
                blocked = bias[...]
                scores = scores * scale + jnp.concatenate([blocked, blocked], axis=1)
                probs = jnp.exp2(scores - lse[index, pair : pair + 1, :])
                grad_probs = dot(v_in[pl.ds(at, TILE), lanes], grad_out, 1, 1)
                grad_scores = (probs * (grad_probs - inner_rows[index, pair : pair + 1, :])).astype(bf16)
                dv[pl.ds(at, TILE), lanes] += dot(probs.astype(bf16), grad_out)
                dk[pl.ds(at, TILE), lanes] += dot(grad_scores, query)
                mixed = dot(key, grad_scores, 0, 0)
                top = pair * 128
                acc[top : top + 64, :] += mixed[:64, :128]
                acc[top + 64 : top + 128, :] += mixed[64:, 128:]
            return inner

        lax.fori_loop(0, tiles, one_tile, 0)
        dq[pl.ds(query_start, BLOCK), :] = (acc[...].T * 0.125).astype(bf16)
        return carry

    lax.fori_loop(0, rows // BLOCK, one_block, 0)
    dk_low = (dk[:rows, :] * 0.125).astype(bf16)
    dv_low = dv[:rows, :].astype(bf16)
    low[...] = dk_low
    weight_grad[0] = dot(own[...], dq[...], 0, 0).astype(bf16)
    weight_grad[1] = dot(other[...], low[...], 0, 0).astype(bf16)
    query_side = sums[...] + dot(dq[...], proj[0], 1, 1)
    source_side = dot(low[...], proj[1], 1, 1)
    if not same:
        own_grad[...] = query_side
        other_grad[...] = source_side
    else:
        sums[...] = query_side + source_side
    low[...] = dv_low
    weight_grad[2] = dot(other[...], low[...], 0, 0).astype(bf16)
    source_side = dot(low[...], proj[2], 1, 1)
    if not same:
        other_grad[...] += source_side
    else:
        own_grad[...] = (sums[...] + source_side).astype(own_grad.dtype)


def attend_backward(grad, resid, norm, own, other, saved, key_col, query_seg, ranges, weights, causal, out_dtype):
    same = other is None
    rows, width = own.shape
    blocks = rows // BLOCK
    ins = [grad, resid, norm, own] + ([] if same else [other])
    ins += [*saved, key_col, query_seg, *weights]
    shapes = [jax.ShapeDtypeStruct((rows, width), out_dtype)]
    if not same:
        shapes.append(jax.ShapeDtypeStruct((rows, width), f32))
    shapes.append(jax.ShapeDtypeStruct((4, width, width), bf16))
    shapes.append(jax.ShapeDtypeStruct((2, width), f32))
    return pl.pallas_call(
        partial(backward_kernel, causal, same),
        out_shape=shapes,
        in_specs=[pl.BlockSpec(memory_space=pltpu.SMEM)] + vmem(len(ins)),
        out_specs=vmem(len(shapes)),
        scratch_shapes=([pltpu.VMEM((rows, width), f32)] if same else [])
        + [
            pltpu.VMEM((rows, width), bf16),
            pltpu.VMEM((blocks, 4, 2 * BLOCK, 128), bf16),
            pltpu.VMEM((blocks, 4, 2 * BLOCK, 128), bf16),
            pltpu.VMEM((blocks, 4, 2 * BLOCK), f32),
            pltpu.VMEM((TILE, BLOCK), f32),
            pltpu.VMEM((width, BLOCK), f32),
            pltpu.VMEM((rows, width), bf16),
            pltpu.VMEM((rows + TILE, width), f32),
            pltpu.VMEM((rows + TILE, width), f32),
        ],
        compiler_params=pltpu.CompilerParams(vmem_limit_bytes=48 * 2**20),
        cost_estimate=cost(10e9, 20e6),
        name="attend_backward",
    )(ranges, *ins)


root_two_pi = 0.7978845608028654
CHUNK = 512


def gelu(pre):
    square = pre * pre
    flat = jnp.tanh(pre * (root_two_pi + (root_two_pi * 0.044715) * square))
    return pre * (0.5 + 0.5 * flat), square, flat


def gelu_slope(pre, square, flat):
    half = 0.5 + 0.5 * flat
    inner = (0.5 * root_two_pi) + (1.5 * root_two_pi * 0.044715) * square
    return half + pre * ((1.0 - flat * flat) * inner)


def ffn_forward_kernel(resid_in, norm_in, up, down, norm_out, resid_out, low_out):
    rows = resid_in.shape[0]

    def one_block(step, carry):
        at = pl.multiple_of(step * TILE, TILE)
        normed, _ = normalise(resid_in[pl.ds(at, TILE), :])
        block = normed * norm_in[0:1, :] + norm_in[1:2, :]
        block_low = block.astype(bf16)
        for chunk in range(up.shape[1] // CHUNK):
            lanes = slice(chunk * CHUNK, (chunk + 1) * CHUNK)
            active, _, _ = gelu(dot(block_low, up[:, lanes]))
            block = block + dot(active.astype(bf16), down[lanes, :])
        resid_out[pl.ds(at, TILE), :] = block
        normed, _ = normalise(block)
        low_out[pl.ds(at, TILE), :] = (normed * norm_out[0:1, :] + norm_out[1:2, :]).astype(bf16)
        return carry

    lax.fori_loop(0, rows // TILE, one_block, 0)


def ffn_forward(resid, norm_in, up, down, norm_out):
    rows, width = resid.shape
    shapes = [jax.ShapeDtypeStruct((rows, width), f32), jax.ShapeDtypeStruct((rows, width), bf16)]
    return pl.pallas_call(
        ffn_forward_kernel,
        out_shape=shapes,
        in_specs=vmem(5),
        out_specs=vmem(2),
        compiler_params=pltpu.CompilerParams(vmem_limit_bytes=32 * 2**20),
        cost_estimate=cost(6e9, 9e6),
        name="ffn_forward",
    )(resid, norm_in, up, down, norm_out)


def ffn_grads(step, active, grad_low, block_low, grad_pre, up_grad, down_grad):
    at = pl.multiple_of(step * CHUNK, CHUNK)
    down_grad[pl.ds(at, CHUNK), :] = dot(active[:, pl.ds(at, CHUNK)], grad_low[...], 0, 0).astype(bf16)
    up_grad[:, pl.ds(at, CHUNK)] = dot(block_low[...], grad_pre[:, pl.ds(at, CHUNK)], 0, 0).astype(bf16)


def ffn_turn_kernel(
    resid_in, norm_in, up, down, norm_out, cotangent, valid,
    final_out, grad_out, up_grad, down_grad, norm_grad,
    active, grad_pre, slopes, grad_low, low,
):
    rows = resid_in.shape[0]
    norm_grad[...] = jnp.zeros(norm_grad.shape, f32)

    def one_block(step, carry):
        at = pl.multiple_of(step * TILE, TILE)
        span = pl.ds(at, TILE)
        normed, _ = normalise(resid_in[span, :])
        block = normed * norm_in[0:1, :] + norm_in[1:2, :]
        block_low = block.astype(bf16)
        low[span, :] = block_low
        for chunk in range(up.shape[1] // CHUNK):
            lanes = slice(chunk * CHUNK, (chunk + 1) * CHUNK)
            pre = dot(block_low, up[:, lanes])
            value, square, flat = gelu(pre)
            value = value.astype(bf16)
            slopes[:, lanes] = gelu_slope(pre, square, flat)
            active[span, lanes] = value
            block = block + dot(value, down[lanes, :])
        normed, scale_inv = normalise(block)
        final_out[span, :] = (normed * norm_out[0:1, :] + norm_out[1:2, :]).astype(bf16)
        grad = cotangent[span, :].astype(f32) * jnp.concatenate([valid[span, :]] * 4, axis=1)
        norm_grad[0:1, :] += jnp.sum(grad * normed, axis=0, keepdims=True)
        norm_grad[1:2, :] += jnp.sum(grad, axis=0, keepdims=True)
        grad = norm_back(grad, normed, scale_inv, norm_out[0:1, :])
        block_grad = grad.astype(bf16)
        grad_low[span, :] = block_grad
        for chunk in range(up.shape[1] // CHUNK):
            lanes = slice(chunk * CHUNK, (chunk + 1) * CHUNK)
            value = (dot(block_grad, down[lanes, :], 1, 1) * slopes[:, lanes]).astype(bf16)
            grad_pre[span, lanes] = value
            grad = grad + dot(value, up[:, lanes], 1, 1)
        grad_out[span, :] = grad
        return carry

    lax.fori_loop(0, rows // TILE, one_block, 0)

    def weights(step, carry):
        ffn_grads(step, active, grad_low, low, grad_pre, up_grad, down_grad)
        return carry

    lax.fori_loop(0, up.shape[1] // CHUNK, weights, 0)


def ffn_turn(resid, norm_in, up, down, norm_out, cotangent, valid):
    rows, width = resid.shape
    hidden = up.shape[1]
    shapes = [
        jax.ShapeDtypeStruct((rows, width), bf16),
        jax.ShapeDtypeStruct((rows, width), f32),
        jax.ShapeDtypeStruct(up.shape, bf16),
        jax.ShapeDtypeStruct(down.shape, bf16),
        jax.ShapeDtypeStruct((2, width), f32),
    ]
    return pl.pallas_call(
        ffn_turn_kernel,
        out_shape=shapes,
        in_specs=vmem(7),
        out_specs=vmem(5),
        scratch_shapes=[
            pltpu.VMEM((rows, hidden), bf16),
            pltpu.VMEM((rows, hidden), bf16),
            pltpu.VMEM((TILE, hidden), f32),
            pltpu.VMEM((rows, width), bf16),
            pltpu.VMEM((rows, width), bf16),
        ],
        compiler_params=pltpu.CompilerParams(vmem_limit_bytes=48 * 2**20),
        cost_estimate=cost(13e9, 18e6),
        name="ffn_turn",
    )(resid, norm_in, up, down, norm_out, cotangent, valid)


def ffn_backward_kernel(
    grad_in, resid_out, norm_out, resid_in, norm_in, up, down,
    grad_out, up_grad, down_grad, norm_grad,
    active, grad_pre, grad_low, low,
):
    rows = resid_in.shape[0]
    norm_grad[...] = jnp.zeros(norm_grad.shape, f32)

    def one_block(step, carry):
        at = pl.multiple_of(step * TILE, TILE)
        span = pl.ds(at, TILE)
        normed, _ = normalise(resid_in[span, :])
        block_low = (normed * norm_in[0:1, :] + norm_in[1:2, :]).astype(bf16)
        low[span, :] = block_low
        normed, scale_inv = normalise(resid_out[span, :])
        grad = grad_in[span, :]
        norm_grad[0:1, :] += jnp.sum(grad * normed, axis=0, keepdims=True)
        norm_grad[1:2, :] += jnp.sum(grad, axis=0, keepdims=True)
        grad = norm_back(grad, normed, scale_inv, norm_out[0:1, :])
        block_grad = grad.astype(bf16)
        grad_low[span, :] = block_grad
        for chunk in range(up.shape[1] // CHUNK):
            lanes = slice(chunk * CHUNK, (chunk + 1) * CHUNK)
            pre = dot(block_low, up[:, lanes])
            value, square, flat = gelu(pre)
            active[span, lanes] = value.astype(bf16)
            slope = gelu_slope(pre, square, flat)
            value = (dot(block_grad, down[lanes, :], 1, 1) * slope).astype(bf16)
            grad_pre[span, lanes] = value
            grad = grad + dot(value, up[:, lanes], 1, 1)
        grad_out[span, :] = grad
        return carry

    lax.fori_loop(0, rows // TILE, one_block, 0)

    def weights(step, carry):
        ffn_grads(step, active, grad_low, low, grad_pre, up_grad, down_grad)
        return carry

    lax.fori_loop(0, up.shape[1] // CHUNK, weights, 0)


def ffn_backward(grad, resid_out, norm_out, resid_in, norm_in, up, down):
    rows, width = resid_in.shape
    hidden = up.shape[1]
    shapes = [
        jax.ShapeDtypeStruct((rows, width), f32),
        jax.ShapeDtypeStruct(up.shape, bf16),
        jax.ShapeDtypeStruct(down.shape, bf16),
        jax.ShapeDtypeStruct((2, width), f32),
    ]
    return pl.pallas_call(
        ffn_backward_kernel,
        out_shape=shapes,
        in_specs=vmem(7),
        out_specs=vmem(4),
        scratch_shapes=[
            pltpu.VMEM((rows, hidden), bf16),
            pltpu.VMEM((rows, hidden), bf16),
            pltpu.VMEM((rows, width), bf16),
            pltpu.VMEM((rows, width), bf16),
        ],
        compiler_params=pltpu.CompilerParams(vmem_limit_bytes=48 * 2**20),
        cost_estimate=cost(11e9, 18e6),
        name="ffn_backward",
    )(grad, resid_out, norm_out, resid_in, norm_in, up, down)


AXES = ("wide", "narrow")


def exchange_phases(mesh):
    devices = list(mesh.devices.reshape(-1))
    count = len(devices)
    bits = [1 << place for place in range(count.bit_length() - 1)]
    spots = [tuple(getattr(device, "coords", None) or ()) for device in devices]
    core, along, across = [], [], []
    for bit in bits:
        moved = [i for i, (p, q) in enumerate(zip(spots[0], spots[bit])) if p != q]
        if spots[0] and not moved:
            core.append(bit)
        elif moved == [2]:
            along.append(bit)
        else:
            across.append(bit)
    phases = []
    for group in (along, across, core):
        phases += [group[i : i + 2] for i in range(0, len(group), 2)]
    return count, bits[::-1], phases


def masks_of(bits):
    masks = [0]
    for bit in bits:
        masks += [mask | bit for mask in masks]
    return masks


def swap(value, count, mask):
    return lax.ppermute(value, AXES, [(i, i ^ mask) for i in range(count)])


def gather_blocks(plan, shard, axis):
    count, order, phases = plan
    me = lax.axis_index(AXES)
    lead, tail = shard.shape[:axis], shard.shape[axis:]
    held = []
    value = shard
    for bits in phases:
        wider = [bit for bit in order if bit in held or bit in bits]
        shape = lead + (2,) * len(wider) + tail
        full = None
        for mask in masks_of(bits):
            piece = swap(value, count, mask) if mask else value
            piece = piece.reshape(lead + tuple(1 if bit in bits else 2 for bit in wider) + tail)
            spot = [0] * len(lead)
            for bit in wider:
                spot.append(jnp.where((me ^ mask) & bit != 0, 1, 0) if bit in bits else 0)
            spot += [0] * len(tail)
            if full is None:
                full = jnp.zeros(shape, shard.dtype)
            full = lax.dynamic_update_slice(full, piece, spot)
        value = full
        held = wider
    return value.reshape(lead + (count * tail[0],) + tail[1:])


def scatter_sums(plan, value, axis):
    count, order, phases = plan
    me = lax.axis_index(AXES)
    lead, tail = value.shape[:axis], value.shape[axis:]
    tail = (tail[0] // count,) + tail[1:]
    held = list(order)
    value = value.reshape(lead + (2,) * len(held) + tail)
    for bits in phases[::-1]:
        left = [bit for bit in held if bit not in bits]
        sizes = lead + tuple(1 if bit in bits else 2 for bit in held) + tail
        total = None
        for mask in masks_of(bits):
            spot = [0] * len(lead)
            for bit in held:
                spot.append(jnp.where((me ^ mask) & bit != 0, 1, 0) if bit in bits else 0)
            spot += [0] * len(tail)
            piece = lax.dynamic_slice(value, spot, sizes).reshape(lead + (2,) * len(left) + tail)
            piece = (swap(piece, count, mask) if mask else piece).astype(f32)
            total = piece if total is None else total + piece
        held = left
        value = total.astype(bf16) if held else total
    return value


def gather_offloaded(shards):
    count = lax.axis_size(AXES)
    flat = [jnp.reshape(item, (-1, 512)) for item in shards]
    whole = lax.all_gather(jnp.concatenate(flat), AXES, axis=0, tiled=False)
    parts = []
    start = 0
    for item, piece in zip(shards, flat):
        stop = start + piece.shape[0]
        block = whole[:, start:stop]
        start = stop
        if item.ndim == 3:
            block = block.reshape(count, item.shape[0], -1, item.shape[2])
            block = jnp.moveaxis(block, 0, 1)
            parts.append(block.reshape(item.shape[0], -1, item.shape[2]))
        else:
            parts.append(block.reshape(-1, item.shape[1]))
    return parts


def scatter_offloaded(grads):
    count = lax.axis_size(AXES)
    flat = []
    for grad in grads:
        if grad.ndim == 3:
            block = grad.reshape(grad.shape[0], count, -1, grad.shape[2])
            block = jnp.moveaxis(block, 1, 0)
        else:
            block = grad
        flat.append(block.reshape(count, -1, 512))
    whole = jnp.concatenate(flat, axis=1)
    whole = lax.psum_scatter(whole, "wide", scatter_dimension=0, tiled=True)
    whole = lax.psum_scatter(whole, "narrow", scatter_dimension=0, tiled=True)[0].astype(f32)
    parts = []
    start = 0
    for grad, block in zip(grads, flat):
        stop = start + block.shape[1]
        if grad.ndim == 3:
            parts.append(whole[start:stop].reshape(grad.shape[0], -1, grad.shape[2]))
        else:
            parts.append(whole[start:stop].reshape(-1, grad.shape[1]))
        start = stop
    return parts


def on_device(
    plan,
    source,
    target,
    source_segments,
    target_segments,
    encoder_proj,
    encoder_mix,
    encoder_up,
    encoder_down,
    self_proj,
    self_mix,
    cross_proj,
    cross_mix,
    decoder_up,
    decoder_down,
    norm_gain,
    norm_bias,
    cotangent,
):
    width = source.shape[-1]
    source_low = source.reshape(-1, width)
    target_low = target.reshape(-1, width)
    enc_mix = gather_blocks(plan, encoder_mix, 0)
    enc_proj = gather_blocks(plan, encoder_proj, 1)
    shard = jnp.stack([norm_gain, norm_bias], axis=1)
    norms = gather_blocks(plan, shard.reshape(1, -1), 0).reshape(-1, 5, 2, norm_gain.shape[1])
    norms = jnp.moveaxis(norms, 0, 2).reshape(5, 2, width).astype(f32)
    own_proj = gather_blocks(plan, self_proj, 1)
    own_mix = gather_blocks(plan, self_mix, 0)
    enc_up = gather_blocks(plan, encoder_up, 0)
    enc_down = gather_blocks(plan, encoder_down, 0)
    far_proj, far_mix, dec_up, dec_down = gather_offloaded(
        [cross_proj, cross_mix, decoder_up, decoder_down]
    )

    source_cols = key_columns(source_segments)
    target_cols = key_columns(target_segments)
    source_rows = source_segments.reshape(-1, 1, BLOCK)
    target_rows = target_segments.reshape(-1, 1, BLOCK)
    enc_ranges = key_ranges(source_segments, source_segments, False)
    own_ranges = key_ranges(target_segments, target_segments, True)
    far_ranges = key_ranges(target_segments, source_segments, False)

    enc_one, _, *enc_saved = attend_forward(
        source_low, None, None, source_cols, source_rows, enc_ranges, (enc_proj, enc_mix), norms[0], False
    )
    own_sum, _, *own_saved = attend_forward(
        target_low, None, None, target_cols, target_rows, own_ranges, (own_proj, own_mix), norms[2], True
    )
    enc_two, enc_low = ffn_forward(enc_one, norms[0], enc_up, enc_down, norms[1])
    far_sum, second_low, *far_saved = attend_forward(
        own_sum, norms[2], enc_low, source_cols, target_rows, far_ranges, (far_proj, far_mix), norms[3], False
    )
    valid = jnp.broadcast_to((target_segments >= 0).reshape(-1, 1).astype(f32), (target_low.shape[0], 128))
    final, grad, dec_up_grad, dec_down_grad, norm_four = ffn_turn(
        far_sum, norms[3], dec_up, dec_down, norms[4], cotangent.reshape(-1, width), valid
    )
    grad, grad_enc, far_grad, norm_three = attend_backward(
        grad, far_sum, norms[3], second_low, enc_low, far_saved, source_cols, target_rows, far_ranges,
        (far_proj, far_mix), False, f32
    )
    far_out, dec_up_out, dec_down_out = scatter_offloaded([far_grad, dec_up_grad, dec_down_grad])
    grad_enc, enc_up_grad, enc_down_grad, norm_one = ffn_backward(
        grad_enc, enc_two, norms[1], enc_one, norms[0], enc_up, enc_down
    )
    enc_up_out = scatter_sums(plan, enc_up_grad, 0)
    enc_down_out = scatter_sums(plan, enc_down_grad, 0)
    target_grad, own_grad, norm_two = attend_backward(
        grad, own_sum, norms[2], target_low, None, own_saved, target_cols, target_rows, own_ranges,
        (own_proj, own_mix), True, bf16
    )
    own_out = scatter_sums(plan, own_grad, 1)
    source_grad, enc_grad, norm_zero = attend_backward(
        grad_enc, enc_one, norms[0], source_low, None, enc_saved, source_cols, source_rows, enc_ranges,
        (enc_proj, enc_mix), False, bf16
    )
    enc_out = scatter_sums(plan, enc_grad, 1)
    norm_grad = jnp.stack([norm_zero, norm_one, norm_two, norm_three, norm_four])
    norm_grad = jnp.moveaxis(norm_grad.reshape(5, 2, -1, norm_gain.shape[1]), 2, 0)
    norm_grad = norm_grad.reshape(norm_grad.shape[0], -1).astype(bf16)
    norm_out = scatter_sums(plan, norm_grad, 0).reshape(5, 2, -1)
    return (
        final.reshape(target.shape),
        source_grad.reshape(source.shape),
        target_grad.reshape(target.shape),
        enc_out[:3],
        enc_out[3],
        enc_up_out,
        enc_down_out,
        own_out[:3],
        own_out[3],
        far_out[:3],
        far_out[3],
        dec_up_out,
        dec_down_out,
        norm_out[:, 0],
        norm_out[:, 1],
    )


def solution(mesh):
    return jax.shard_map(
        partial(on_device, exchange_phases(mesh)),
        mesh=mesh,
        in_specs=(
            P(("wide", "narrow"), None, None),
            P(("wide", "narrow"), None, None),
            P(("wide", "narrow"), None),
            P(("wide", "narrow"), None),
            P(None, ("wide", "narrow"), None),
            P(("wide", "narrow"), None),
            P(("wide", "narrow"), None),
            P(("wide", "narrow"), None),
            P(None, ("wide", "narrow"), None),
            P(("wide", "narrow"), None),
            P(None, ("wide", "narrow"), None),
            P(("wide", "narrow"), None),
            P(("wide", "narrow"), None),
            P(("wide", "narrow"), None),
            P(None, ("wide", "narrow")),
            P(None, ("wide", "narrow")),
            P(("wide", "narrow"), None, None),
        ),
        out_specs=(
            P(("wide", "narrow"), None, None),
            P(("wide", "narrow"), None, None),
            P(("wide", "narrow"), None, None),
            P(None, ("wide", "narrow"), None),
            P(("wide", "narrow"), None),
            P(("wide", "narrow"), None),
            P(("wide", "narrow"), None),
            P(None, ("wide", "narrow"), None),
            P(("wide", "narrow"), None),
            P(None, ("wide", "narrow"), None),
            P(("wide", "narrow"), None),
            P(("wide", "narrow"), None),
            P(("wide", "narrow"), None),
            P(None, ("wide", "narrow")),
            P(None, ("wide", "narrow")),
        ),
        check_vma=False,
    )
```

time: 1020 us -> 537 us (0.53)
  matrix products: 339 us -> 0 us
  Pallas kernels: 0 us -> 201 us
  waiting for transfers between devices: 286 us -> 121 us
  local copies, waits for them, and re-layouts: 184 us -> 72.8 us
  starting transfers between devices: 0.16 us -> 97.4 us
  other arithmetic: 109 us -> 22.9 us
  blocking collectives: 72.8 us -> 0 us
  loops' own time: 10.3 us -> 0 us
    dot_general x90 -> x0, matrix products: 339 us -> none  [the longest x12 91.6 us: block_scores(): jnp.einsum('qhd,khd->hqk', query_block, key_row, preferred_element_type=j...]
    pallas_call x0 -> x9, Pallas kernels: none -> 201 us  [the longest x3 80.8 us: attend_backward(): pl.pallas_call(partial(backward_kernel, causal, same), out_shape=shapes,...]
    reduce_scatter x2, waiting for transfers between devices: 137 us -> 0.14 us  [the longest x1 0.12 us: scatter_offloaded(): lax.psum_scatter(whole, 'narrow', scatter_dimension=0, tiled=True)[0]]
    unnamed x5 -> x3, waiting for transfers between devices: 123 us -> 0.05 us
    ppermute x0 -> x84, waiting for transfers between devices: none -> 121 us  [swap(): return lax.ppermute(value, AXES, [(i, i ^ mask) for i in range(count)])]
    ppermute x0 -> x84, starting transfers between devices: none -> 97.3 us  [swap(): return lax.ppermute(value, AXES, [(i, i ^ mask) for i in range(count)])]
    all_gather x1 -> x0, blocking collectives: 72.8 us -> none  [on_device(): lax.all_gather(jnp.concatenate([norm_gain, norm_bias]), ('wide', 'narrow'...]
    reduce_sum x18 -> x2, other arithmetic: 46.4 us -> 1.62 us  [the longest x1 1.36 us: key_ranges(): real = jnp.sum((key_order < big).astype(jnp.int32))]
  transfers between devices with their start and end apart: 4 -> 87, of which waited for: 4 -> 30; matrix products, arithmetic and copies ran while one was open for 2% -> 7% of each run, Pallas kernels for 0% -> 23%
where the time goes in v2:
time: 537 us; the launch traced here: 531 us
  Pallas kernels  201 us (37%)
  waiting for transfers between devices  121 us (23%)
  starting transfers between devices  97.4 us (18%)
  local copies, waits for them, and re-layouts  72.8 us (14%)
  other arithmetic  22.9 us (4%)
  between operations  15.6 us (3%)
    ppermute x84, waiting for transfers between devices, swap(): return lax.ppermute(value, AXES, [(i, i ^ mask) for i in range(count)])  121 us
    ppermute x84, starting transfers between devices, swap(): return lax.ppermute(value, AXES, [(i, i ^ mask) for i in range(count)])  97.3 us
    pallas_call x3, Pallas kernels, attend_backward(): pl.pallas_call(partial(backward_kernel, causal, same), out_shape=shapes,...  80.8 us
    pallas_call x3, Pallas kernels, attend_forward(): pl.pallas_call(partial(forward_kernel, causal, fresh), out_shape=shapes,...  62.5 us
    unnamed x116, local copies, waits for them, and re-layouts  30.6 us
    pallas_call x1, Pallas kernels, ffn_turn(): pl.pallas_call(ffn_turn_kernel, out_shape=shapes, in_specs=vmem(7), out_s...  25.4 us
    pallas_call x1, Pallas kernels, ffn_backward(): pl.pallas_call(ffn_backward_kernel, out_shape=shapes, in_specs=vmem(7), o...  23.1 us
  transfers between devices with their start and end apart: 87, of which 30 were waited for; matrix products, arithmetic and copies ran while one was open for 7% of the time, Pallas kernels for 23%

profile of v2, /device:TPU:0, one launch (start us, length us, event | category | flops | bytes accessed | tf_op | source)
XLA Modules:
  0.0 530.5 jit_solution(727389316259135862)
XLA Ops:
  8.1 5.0 collective-permute-start.16
  15.2 2.4 collective-permute-start.30
  38.0 2.4 collective-permute-start.19
  43.7 2.4 collective-permute-start.9
  46.9 5.3 %collective-permute-done.8 = bf16[16,512]{1,0:T(8,128)(2,1)S(1)} collective-permute-done((bf16[16,512]{1,0:T(8,128)(2,1)S(1)}, bf16[16,512]{1,0:T(8,128)(2,1)S(1)}, u32[]{:S(2)}, u32[]{:S(2)}) %collective-permute-start.8) | collective-permute-done | bytes 16416 | tf_op jit(solution)/shard_map/ppermute | solution.py:595
  58.2 2.5 collective-permute-done
  60.8 3.0 collective-permute-start.1
  63.8 3.1 collective-permute-done.1
  68.0 2.3 collective-permute-start.37
  75.3 9.0 %collective-permute-done.36 = bf16[16,2048]{1,0:T(8,128)(2,1)S(1)} collective-permute-done((bf16[16,2048]{1,0:T(8,128)(2,1)S(1)}, bf16[16,2048]{1,0:T(8,128)(2,1)S(1)}, u32[]{:S(2)}, u32[]{:S(2)}) %collective-permute-start.36) | collective-permute-done | bytes 65568 | tf_op jit(solution)/shard_map/ppermute | solution.py:595
  84.3 4.1 collective-permute-start.33
  88.5 5.7 %collective-permute-done.43 = bf16[64,512]{1,0:T(8,128)(2,1)S(1)} collective-permute-done((bf16[64,512]{1,0:T(8,128)(2,1)S(1)}, bf16[64,512]{1,0:T(8,128)(2,1)S(1)}, u32[]{:S(2)}, u32[]{:S(2)}) %collective-permute-start.43) | collective-permute-done | bytes 65568 | tf_op jit(solution)/shard_map/ppermute | solution.py:595
  95.8 2.8 collective-permute-start.12
  99.9 2.9 collective-permute-done.10
  102.9 6.9 %collective-permute-done.11 = bf16[2,2,16,512]{3,2,1,0:T(8,128)(2,1)S(1)} collective-permute-done((bf16[2,2,16,512]{3,2,1,0:T(8,128)(2,1)S(1)}, bf16[2,2,16,512]{3,2,1,0:T(8,128)(2,1)S(1)}, u32[]{:S(2)}, u32[]{:S(2)}) %collective-permute-start.11) | collective-permute-done | bytes 65568 | tf_op jit(solution)/shard_map/ppermute | solution.py:595
  109.8 2.3 collective-permute-start.25
  115.3 7.8 %collective-permute-done.3 = bf16[3,2,2,16,512]{4,3,2,1,0:T(8,128)(2,1)S(1)} collective-permute-done((bf16[3,2,2,16,512]{4,3,2,1,0:T(8,128)(2,1)S(1)}, bf16[3,2,2,16,512]{4,3,2,1,0:T(8,128)(2,1)S(1)}, u32[]{:S(2)}, u32[]{:S(2)}) %collective-permute-start.3) | collective-permute-done | bytes 196640 | tf_op jit(solution)/shard_map/ppermute | solution.py:595
  124.5 11.6 %collective-permute-done.4 = bf16[3,2,2,16,512]{4,3,2,1,0:T(8,128)(2,1)S(1)} collective-permute-done((bf16[3,2,2,16,512]{4,3,2,1,0:T(8,128)(2,1)S(1)}, bf16[3,2,2,16,512]{4,3,2,1,0:T(8,128)(2,1)S(1)}, u32[]{:S(2)}, u32[]{:S(2)}) %collective-permute-start.4) | collective-permute-done | bytes 196640 | tf_op jit(solution)/shard_map/ppermute | solution.py:595
  142.9 3.4 collective-permute-done.38
  148.3 4.4 collective-permute-done.45
  156.5 22.2 %attend_forward.4 = (f32[1024,512]{1,0:T(8,128)S(1)}, bf16[1024,512]{1,0:T(8,128)(2,1)}, bf16[1024,512]{1,0:T(8,128)(2,1)S(1)}, bf16[1280,512]{1,0:T(8,128)(2,1)...) custom-call(s32[3,8]{1,0:T(4,128)S(1)} %pad_add_fusion.2.ranges, ...), custom_call_target="tpu_custom_call" | custom-call | flops 4000000000 | bytes 12000000 | tf_op jit(solution)/shard_map/attend_forward/pallas_call | solution.py:208
  183.1 18.0 %attend_forward.3 = (f32[1024,512]{1,0:T(8,128)S(1)}, bf16[1024,512]{1,0:T(8,128)(2,1)}, bf16[1024,512]{1,0:T(8,128)(2,1)S(1)}, bf16[1280,512]{1,0:T(8,128)(2,1)...) custom-call(s32[3,8]{1,0:T(4,128)S(1)} %pad_add_fusion.1.ranges, ...), custom_call_target="tpu_custom_call" | custom-call | flops 4000000000 | bytes 12000000 | tf_op jit(solution)/shard_map/attend_forward/pallas_call | solution.py:208
  207.2 8.9 %ffn_forward.1 = (f32[1024,512]{1,0:T(8,128)S(1)}, bf16[1024,512]{1,0:T(8,128)(2,1)S(1)}) custom-call(f32[1024,512]{1,0:T(8,128)S(1)} %get-tuple-element.56.resid_in.refs_1_, f32[2,512]{1,0:T(2,128)S(1)} %squeeze.38.refs_5_.norm_in.refs_2_, bf16[512,2048]{1,0:T(8,128)(2,1)S(1)} %bitcast.483, bf16[2048,512]{1,0:T(8,128)(2,1)S(1)} %bitcast.481, ...), custom_call_target="tpu_custom_call" | custom-call | flops 6000000000 | bytes 9000000 | tf_op jit(solution)/shard_map/ffn_forward/pallas_call | solution.py:403
  222.6 4.7 fusion.54
  227.5 4.7 reshape.1247.up
  235.1 22.2 %attend_forward.5 = (f32[1024,512]{1,0:T(8,128)S(1)}, bf16[1024,512]{1,0:T(8,128)(2,1)S(1)}, bf16[1024,512]{1,0:T(8,128)(2,1)S(1)}, bf16[1280,512]{1,0:T(8,128)(...) custom-call(s32[3,8]{1,0:T(4,128)S(1)} %pad_add_fusion.ranges, ...), custom_call_target="tpu_custom_call" | custom-call | flops 4000000000 | bytes 12000000 | tf_op jit(solution)/shard_map/attend_forward/pallas_call | solution.py:208
  261.0 25.4 %ffn_turn.1 = (bf16[1024,512]{1,0:T(8,128)(2,1)}, f32[1024,512]{1,0:T(8,128)S(1)}, bf16[512,2048]{1,0:T(8,128)(2,1)S(1)}, bf16[2048,512]{1,0:T(8,128)(2,1)}, f32[2,512]{1,0:T(2,128)S(1)}) custom-call(f32[1024,512]{1,0:T(8,128)} %copy-done.20, f32[2,512]{1,0:T(2,128)S(1)} %squeeze.40.refs_7_.norm_in.refs_2_, bf16[512,2048]{1,0:T(8,128)(2,1)} %reshape.1247.up, ...), custom_call_target="tpu_custom_call" | custom-call | flops 12999999488 | bytes 18000000 | tf_op jit(solution)/shard_map/ffn_turn/pallas_call | solution.py:478
  287.8 29.2 %attend_backward.3 = (f32[1024,512]{1,0:T(8,128)}, f32[1024,512]{1,0:T(8,128)}, bf16[4,512,512]{2,1,0:T(8,128)(2,1)}, f32[2,512]{1,0:T(2,128)S(1)}) custom-call(s32[3,8]{1,0:T(4,128)S(1)} %pad_add_fusion.ranges, f32[1024,512]{1,0:T(8,128)} %copy-done.42, f32[1024,512]{1,0:T(8,128)} %copy-done.20, f32[2,512]{1,0:T(2,128)S(1)} %squeeze.40.refs_7_.norm_in.refs_2_, ...), custom_call_target="tpu_custom_call" | custom-call | flops 10000000000 | bytes 20000000 | tf_op jit(solution)/shard_map/attend_backward/pallas_call | solution.py:341
  316.9 3.2 copy.165
  320.1 2.5 reshape.1287
  322.7 6.3 %pad_maximum_fusion = bf16[32,192,512]{2,1,0:T(8,128)(2,1)} fusion(bf16[32,64,512]{2,1,0:T(8,128)(2,1)} %bitcast.520, bf16[32,64,512]{2,1,0:T(8,128)(2,1)} %reshape.1287, bf16[32,64,512]{2,1,0:T(8,128)(2,1)} %bitcast.510), kind=kLoop, calls=%fused_computation | loop fusion | flops 18874368 | bytes 12582912 | tf_op jit(solution)/shard_map/concatenate | solution.py:676
  334.5 24.6 %attend_backward.5 = (bf16[1024,512]{1,0:T(8,128)(2,1)}, bf16[4,512,512]{2,1,0:T(8,128)(2,1)}, f32[2,512]{1,0:T(2,128)S(1)}) custom-call(s32[3,8]{1,0:T(4,128)S(1)} %pad_add_fusion.1.ranges, f32[1024,512]{1,0:T(8,128)} %get-tuple-element.76.refs_0_, f32[1024,512]{1,0:T(8,128)} %copy-done.18, f32[2,512]{1,0:T(2,128)S(1)} %squeeze.18.refs_5_.refs_1_.refs_2_, ...), custom_call_target="tpu_custom_call" | custom-call | flops 10000000000 | bytes 20000000 | tf_op jit(solution)/shard_map/attend_backward/pallas_call | solution.py:341
  359.1 23.1 %ffn_backward.1 = (f32[1024,512]{1,0:T(8,128)S(1)}, bf16[512,2048]{1,0:T(8,128)(2,1)S(1)}, bf16[2048,512]{1,0:T(8,128)(2,1)}, f32[2,512]{1,0:T(2,128)S(1)}) custom-call(f32[1024,512]{1,0:T(8,128)} %get-tuple-element.67.grad_in, f32[1024,512]{1,0:T(8,128)} %copy-done.41, f32[2,512]{1,0:T(2,128)S(1)} %squeeze.39.norm_out, f32[1024,512]{1,0:T(8,128)} %copy-done.21, ...), custom_call_target="tpu_custom_call" | custom-call | flops 11000000512 | bytes 18000000 | tf_op jit(solution)/shard_map/ffn_backward/pallas_call | solution.py:547
  383.6 27.0 %attend_backward.4 = (bf16[1024,512]{1,0:T(8,128)(2,1)}, bf16[4,512,512]{2,1,0:T(8,128)(2,1)}, f32[2,512]{1,0:T(2,128)S(1)}) custom-call(s32[3,8]{1,0:T(4,128)S(1)} %pad_add_fusion.2.ranges, f32[1024,512]{1,0:T(8,128)} %copy-done.43, f32[1024,512]{1,0:T(8,128)} %copy-done.21, f32[2,512]{1,0:T(2,128)S(1)} %squeeze.38.refs_5_.norm_in.refs_2_, ...), custom_call_target="tpu_custom_call" | custom-call | flops 10000000000 | bytes 20000000 | tf_op jit(solution)/shard_map/attend_backward/pallas_call | solution.py:341
  417.2 3.1 collective-permute-start.79
  424.1 3.4 collective-permute-start.82
  444.7 3.1 collective-permute-done.66
  450.2 8.2 %collective-permute-done.71 = bf16[4,2,2,16,512]{4,3,0,2,1:T(8,128)(2,1)S(1)} collective-permute-done((bf16[4,2,2,16,512]{4,3,0,2,1:T(8,128)(2,1)S(1)}, bf16[4,2,2,16,512]{4,3,0,2,1:T(8,128)(2,1)S(1)}, u32[]{:S(2)}, u32[]{:S(2)}) %collective-permute-start.71) | collective-permute-done | bytes 262176 | tf_op jit(solution)/shard_map/ppermute | solution.py:595
  459.6 9.6 %collective-permute-done.73 = bf16[4,2,2,16,512]{4,3,0,2,1:T(8,128)(2,1)S(1)} collective-permute-done((bf16[4,2,2,16,512]{4,3,0,2,1:T(8,128)(2,1)S(1)}, bf16[4,2,2,16,512]{4,3,0,2,1:T(8,128)(2,1)S(1)}, u32[]{:S(2)}, u32[]{:S(2)}) %collective-permute-start.73) | collective-permute-done | bytes 262176 | tf_op jit(solution)/shard_map/ppermute | solution.py:595
  475.1 3.4 collective-permute-start.69
  478.9 3.5 collective-permute-done.52
  482.4 3.5 collective-permute-done.51
  487.0 3.1 collective-permute-start.76
  492.1 3.0 collective-permute-done.76
  495.1 2.4 collective-permute-start.55
  497.5 7.3 %collective-permute-done.75 = bf16[4,16,512]{2,1,0:T(8,128)(2,1)S(1)} collective-permute-done((bf16[4,16,512]{2,1,0:T(8,128)(2,1)S(1)}, bf16[4,16,512]{2,1,0:T(8,128)(2,1)S(1)}, u32[]{:S(2)}, u32[]{:S(2)}) %collective-permute-start.75) | collective-permute-done | bytes 65568 | tf_op jit(solution)/shard_map/ppermute | solution.py:595
  505.4 2.9 collective-permute-start.61
  508.4 7.1 %collective-permute-done.54 = bf16[4,16,512]{2,1,0:T(8,128)(2,1)S(1)} collective-permute-done((bf16[4,16,512]{2,1,0:T(8,128)(2,1)S(1)}, bf16[4,16,512]{2,1,0:T(8,128)(2,1)S(1)}, u32[]{:S(2)}, u32[]{:S(2)}) %collective-permute-start.54) | collective-permute-done | bytes 65568 | tf_op jit(solution)/shard_map/ppermute | solution.py:595
  (444 shorter events, 139.8 us)
Async XLA Ops:
  7.3 212.6 %all-gather.3.cloned.1.call-start = ((), (), s32[]{:S(2)}) async-start(), calls=%async_computation.4 | async-start | bytes 6488064 | tf_op jit(solution)/shard_map/all_gather | solution.py:650
  8.1 22.6 %collective-permute-start.16 = (bf16[1,160]{1,0:T(2,128)(2,1)S(1)}, bf16[1,160]{1,0:T(2,128)(2,1)S(1)}, u32[]{:S(2)}, u32[]{:S(2)}) collective-permute-start(bf16[1,160]{1,0:T(2,128)(2,1)S(1)} %reshape.1184), channel_id=1, source_target_pairs={{0,3},{1,2},{2,1},{3,0},{4,7},{5,6},{6,5},{7,4},{8,11},{9,10},{10,... | collective-permute-start | bytes 968 | tf_op jit(solution)/shard_map/ppermute | solution.py:595
  13.2 16.0 %collective-permute-start.15 = (bf16[1,160]{1,0:T(2,128)(2,1)S(1)}, bf16[1,160]{1,0:T(2,128)(2,1)S(1)}, u32[]{:S(2)}, u32[]{:S(2)}) collective-permute-start(bf16[1,160]{1,0:T(2,128)(2,1)S(1)} %reshape.1184), channel_id=1, source_target_pairs={{0,2},{1,3},{2,0},{3,1},{4,6},{5,7},{6,4},{7,5},{8,10},{9,11},{10,... | collective-permute-start | bytes 968 | tf_op jit(solution)/shard_map/ppermute | solution.py:595
  13.2 15.3 %collective-permute-start.14 = (bf16[1,160]{1,0:T(2,128)(2,1)S(1)}, bf16[1,160]{1,0:T(2,128)(2,1)S(1)}, u32[]{:S(2)}, u32[]{:S(2)}) collective-permute-start(bf16[1,160]{1,0:T(2,128)(2,1)S(1)} %reshape.1184), channel_id=1, source_target_pairs={{0,1},{1,0},{2,3},{3,2},{4,5},{5,4},{6,7},{7,6},{8,9},{9,8},{10,11... | collective-permute-start | bytes 968 | tf_op jit(solution)/shard_map/ppermute | solution.py:595
  13.8 39.8 %collective-permute-start.28 = (bf16[16,512]{1,0:T(8,128)(2,1)}, bf16[16,512]{1,0:T(8,128)(2,1)S(1)}, u32[]{:S(2)}, u32[]{:S(2)}) collective-permute-start(bf16[16,512]{1,0:T(8,128)(2,1)} %param.22), channel_id=1, source_target_pairs={{0,1},{1,0},{2,3},{3,2},{4,5},{5,4},{6,7},{7,6},{8,9},{9,8},{10,11... | collective-permute-start | bytes 49160 | tf_op jit(solution)/shard_map/ppermute | solution.py:595
  15.2 41.7 %collective-permute-start.30 = (bf16[16,512]{1,0:T(8,128)(2,1)}, bf16[16,512]{1,0:T(8,128)(2,1)S(1)}, u32[]{:S(2)}, u32[]{:S(2)}) collective-permute-start(bf16[16,512]{1,0:T(8,128)(2,1)} %param.22), channel_id=1, source_target_pairs={{0,3},{1,2},{2,1},{3,0},{4,7},{5,6},{6,5},{7,4},{8,11},{9,10},{10,... | collective-permute-start | bytes 49160 | tf_op jit(solution)/shard_map/ppermute | solution.py:595
  20.1 466.7 %reduce-scatter.3.cloned.1.call-start = ((), (), s32[]{:S(2)}) async-start(), calls=%async_computation.2 | async-start | bytes 7077888 | tf_op jit(solution)/shard_map/reduce_scatter | solution.py:677
  28.5 27.3 %collective-permute-start.29 = (bf16[16,512]{1,0:T(8,128)(2,1)S(1)}, bf16[16,512]{1,0:T(8,128)(2,1)S(1)}, u32[]{:S(2)}, u32[]{:S(2)}) collective-permute-start(bf16[16,512]{1,0:T(8,128)(2,1)S(1)} %copy-done.52), channel_id=1, source_target_pairs={{0,2},{1,3},{2,0},{3,1},{4,6},{5,7},{6,4},{7,5},{8,10},{9,11},{10,... | collective-permute-start | bytes 49160 | tf_op jit(solution)/shard_map/ppermute | solution.py:595
  29.2 17.6 %collective-permute-start.7 = (bf16[16,512]{1,0:T(8,128)(2,1)S(1)}, bf16[16,512]{1,0:T(8,128)(2,1)S(1)}, u32[]{:S(2)}, u32[]{:S(2)}) collective-permute-start(bf16[16,512]{1,0:T(8,128)(2,1)S(1)} %copy-done.51), channel_id=1, source_target_pairs={{0,1},{1,0},{2,3},{3,2},{4,5},{5,4},{6,7},{7,6},{8,9},{9,8},{10,11... | collective-permute-start | bytes 49160 | tf_op jit(solution)/shard_map/ppermute | solution.py:595
  52.2 18.2 %collective-permute-start.21 = (bf16[3,16,512]{2,1,0:T(8,128)(2,1)S(1)}, bf16[3,16,512]{2,1,0:T(8,128)(2,1)S(1)}, u32[]{:S(2)}, u32[]{:S(2)}) collective-permute-start(bf16[3,16,512]{2,1,0:T(8,128)(2,1)S(1)} %copy-done.50), channel_id=1, source_target_pairs={{0,1},{1,0},{2,3},{3,2},{4,5},{5,4},{6,7},{7,6},{8,9},{9,8},{10,11... | collective-permute-start | bytes 147464 | tf_op jit(solution)/shard_map/ppermute | solution.py:595
  52.2 20.5 %collective-permute-start.23 = (bf16[3,16,512]{2,1,0:T(8,128)(2,1)S(1)}, bf16[3,16,512]{2,1,0:T(8,128)(2,1)S(1)}, u32[]{:S(2)}, u32[]{:S(2)}) collective-permute-start(bf16[3,16,512]{2,1,0:T(8,128)(2,1)S(1)} %copy-done.50), channel_id=1, source_target_pairs={{0,3},{1,2},{2,1},{3,0},{4,7},{5,6},{6,5},{7,4},{8,11},{9,10},{10,... | collective-permute-start | bytes 147464 | tf_op jit(solution)/shard_map/ppermute | solution.py:595
  53.6 17.0 %collective-permute-start.22 = (bf16[3,16,512]{2,1,0:T(8,128)(2,1)S(1)}, bf16[3,16,512]{2,1,0:T(8,128)(2,1)S(1)}, u32[]{:S(2)}, u32[]{:S(2)}) collective-permute-start(bf16[3,16,512]{2,1,0:T(8,128)(2,1)S(1)} %copy-done.50), channel_id=1, source_target_pairs={{0,2},{1,3},{2,0},{3,1},{4,6},{5,7},{6,4},{7,5},{8,10},{9,11},{10,... | collective-permute-start | bytes 147464 | tf_op jit(solution)/shard_map/ppermute | solution.py:595
  68.0 30.5 %collective-permute-start.37 = (bf16[16,2048]{1,0:T(8,128)(2,1)S(1)}, bf16[16,2048]{1,0:T(8,128)(2,1)S(1)}, u32[]{:S(2)}, u32[]{:S(2)}) collective-permute-start(bf16[16,2048]{1,0:T(8,128)(2,1)S(1)} %copy-done.48), channel_id=1, source_target_pairs={{0,3},{1,2},{2,1},{3,0},{4,7},{5,6},{6,5},{7,4},{8,11},{9,10},{10,... | collective-permute-start | bytes 196616 | tf_op jit(solution)/shard_map/ppermute | solution.py:595
  70.4 13.8 %collective-permute-start.36 = (bf16[16,2048]{1,0:T(8,128)(2,1)S(1)}, bf16[16,2048]{1,0:T(8,128)(2,1)S(1)}, u32[]{:S(2)}, u32[]{:S(2)}) collective-permute-start(bf16[16,2048]{1,0:T(8,128)(2,1)S(1)} %copy-done.48), channel_id=1, source_target_pairs={{0,2},{1,3},{2,0},{3,1},{4,6},{5,7},{6,4},{7,5},{8,10},{9,11},{10,... | collective-permute-start | bytes 196616 | tf_op jit(solution)/shard_map/ppermute | solution.py:595
  70.6 17.7 %collective-permute-start.42 = (bf16[64,512]{1,0:T(8,128)(2,1)S(1)}, bf16[64,512]{1,0:T(8,128)(2,1)S(1)}, u32[]{:S(2)}, u32[]{:S(2)}) collective-permute-start(bf16[64,512]{1,0:T(8,128)(2,1)S(1)} %copy-done.47), channel_id=1, source_target_pairs={{0,1},{1,0},{2,3},{3,2},{4,5},{5,4},{6,7},{7,6},{8,9},{9,8},{10,11... | collective-permute-start | bytes 196616 | tf_op jit(solution)/shard_map/ppermute | solution.py:595
  72.8 23.0 %collective-permute-start.44 = (bf16[64,512]{1,0:T(8,128)(2,1)S(1)}, bf16[64,512]{1,0:T(8,128)(2,1)S(1)}, u32[]{:S(2)}, u32[]{:S(2)}) collective-permute-start(bf16[64,512]{1,0:T(8,128)(2,1)S(1)} %copy-done.47), channel_id=1, source_target_pairs={{0,3},{1,2},{2,1},{3,0},{4,7},{5,6},{6,5},{7,4},{8,11},{9,10},{10,... | collective-permute-start | bytes 196616 | tf_op jit(solution)/shard_map/ppermute | solution.py:595
  75.2 19.0 %collective-permute-start.43 = (bf16[64,512]{1,0:T(8,128)(2,1)S(1)}, bf16[64,512]{1,0:T(8,128)(2,1)S(1)}, u32[]{:S(2)}, u32[]{:S(2)}) collective-permute-start(bf16[64,512]{1,0:T(8,128)(2,1)S(1)} %copy-done.47), channel_id=1, source_target_pairs={{0,2},{1,3},{2,0},{3,1},{4,6},{5,7},{6,4},{7,5},{8,10},{9,11},{10,... | collective-permute-start | bytes 196616 | tf_op jit(solution)/shard_map/ppermute | solution.py:595
  84.3 29.5 %collective-permute-start.33 = (bf16[2,2,16,512]{3,2,1,0:T(8,128)(2,1)S(1)}, bf16[2,2,16,512]{3,2,1,0:T(8,128)(2,1)S(1)}, u32[]{:S(2)}, u32[]{:S(2)}) collective-permute-start(bf16[2,2,16,512]{3,2,1,0:T(8,128)(2,1)S(1)} %constant_dynamic-update-slice_fusion), channel_id=1, source_target_pairs={{0,24},{1,25},{2,26},{3,27},{4,28},{5,29},{6,30},{7,31},{8,16},{9,... | collective-permute-start | bytes 196616 | tf_op jit(solution)/shard_map/ppermute | solution.py:595
  88.4 25.1 %collective-permute-start.32 = (bf16[2,2,16,512]{3,2,1,0:T(8,128)(2,1)S(1)}, bf16[2,2,16,512]{3,2,1,0:T(8,128)(2,1)S(1)}, u32[]{:S(2)}, u32[]{:S(2)}) collective-permute-start(bf16[2,2,16,512]{3,2,1,0:T(8,128)(2,1)S(1)} %constant_dynamic-update-slice_fusion), channel_id=1, source_target_pairs={{0,16},{1,17},{2,18},{3,19},{4,20},{5,21},{6,22},{7,23},{8,24},{9,... | collective-permute-start | bytes 196616 | tf_op jit(solution)/shard_map/ppermute | solution.py:595
  94.2 18.0 %collective-permute-start.31 = (bf16[2,2,16,512]{3,2,1,0:T(8,128)(2,1)S(1)}, bf16[2,2,16,512]{3,2,1,0:T(8,128)(2,1)S(1)}, u32[]{:S(2)}, u32[]{:S(2)}) collective-permute-start(bf16[2,2,16,512]{3,2,1,0:T(8,128)(2,1)S(1)} %constant_dynamic-update-slice_fusion), channel_id=1, source_target_pairs={{0,8},{1,9},{2,10},{3,11},{4,12},{5,13},{6,14},{7,15},{8,0},{9,1},... | collective-permute-start | bytes 196616 | tf_op jit(solution)/shard_map/ppermute | solution.py:595
  95.8 14.0 %collective-permute-start.12 = (bf16[2,2,16,512]{3,2,1,0:T(8,128)(2,1)S(1)}, bf16[2,2,16,512]{3,2,1,0:T(8,128)(2,1)S(1)}, u32[]{:S(2)}, u32[]{:S(2)}) collective-permute-start(bf16[2,2,16,512]{3,2,1,0:T(8,128)(2,1)S(1)} %constant_dynamic-update-slice_fusion.10), channel_id=1, source_target_pairs={{0,24},{1,25},{2,26},{3,27},{4,28},{5,29},{6,30},{7,31},{8,16},{9,... | collective-permute-start | bytes 196616 | tf_op jit(solution)/shard_map/ppermute | solution.py:595
  109.8 32.0 %collective-permute-start.26 = (bf16[3,2,2,16,512]{4,3,2,1,0:T(8,128)(2,1)S(1)}, bf16[3,2,2,16,512]{4,3,2,1,0:T(8,128)(2,1)S(1)}, u32[]{:S(2)}, u32[]{:S(2)}) collective-permute-start(bf16[3,2,2,16,512]{4,3,2,1,0:T(8,128)(2,1)S(1)} %bitcast_dynamic-update-slice_fusion.44), channel_id=1, source_target_pairs={{0,24},{1,25},{2,26},{3,27},{4,28},{5,29},{6,30},{7,31},{8,16},{9,... | collective-permute-start | bytes 589832 | tf_op jit(solution)/shard_map/ppermute | solution.py:595
  109.8 30.0 %collective-permute-start.25 = (bf16[3,2,2,16,512]{4,3,2,1,0:T(8,128)(2,1)S(1)}, bf16[3,2,2,16,512]{4,3,2,1,0:T(8,128)(2,1)S(1)}, u32[]{:S(2)}, u32[]{:S(2)}) collective-permute-start(bf16[3,2,2,16,512]{4,3,2,1,0:T(8,128)(2,1)S(1)} %bitcast_dynamic-update-slice_fusion.44), channel_id=1, source_target_pairs={{0,16},{1,17},{2,18},{3,19},{4,20},{5,21},{6,22},{7,23},{8,24},{9,... | collective-permute-start | bytes 589832 | tf_op jit(solution)/shard_map/ppermute | solution.py:595
  112.1 26.4 %collective-permute-start.24 = (bf16[3,2,2,16,512]{4,3,2,1,0:T(8,128)(2,1)S(1)}, bf16[3,2,2,16,512]{4,3,2,1,0:T(8,128)(2,1)S(1)}, u32[]{:S(2)}, u32[]{:S(2)}) collective-permute-start(bf16[3,2,2,16,512]{4,3,2,1,0:T(8,128)(2,1)S(1)} %bitcast_dynamic-update-slice_fusion.44), channel_id=1, source_target_pairs={{0,8},{1,9},{2,10},{3,11},{4,12},{5,13},{6,14},{7,15},{8,0},{9,1},... | collective-permute-start | bytes 589832 | tf_op jit(solution)/shard_map/ppermute | solution.py:595
  113.5 24.5 %collective-permute-start.5 = (bf16[3,2,2,16,512]{4,3,2,1,0:T(8,128)(2,1)S(1)}, bf16[3,2,2,16,512]{4,3,2,1,0:T(8,128)(2,1)S(1)}, u32[]{:S(2)}, u32[]{:S(2)}) collective-permute-start(bf16[3,2,2,16,512]{4,3,2,1,0:T(8,128)(2,1)S(1)} %bitcast_dynamic-update-slice_fusion.48), channel_id=1, source_target_pairs={{0,24},{1,25},{2,26},{3,27},{4,28},{5,29},{6,30},{7,31},{8,16},{9,... | collective-permute-start | bytes 589832 | tf_op jit(solution)/shard_map/ppermute | solution.py:595
  123.1 13.0 %collective-permute-start.4 = (bf16[3,2,2,16,512]{4,3,2,1,0:T(8,128)(2,1)S(1)}, bf16[3,2,2,16,512]{4,3,2,1,0:T(8,128)(2,1)S(1)}, u32[]{:S(2)}, u32[]{:S(2)}) collective-permute-start(bf16[3,2,2,16,512]{4,3,2,1,0:T(8,128)(2,1)S(1)} %bitcast_dynamic-update-slice_fusion.48), channel_id=1, source_target_pairs={{0,16},{1,17},{2,18},{3,19},{4,20},{5,21},{6,22},{7,23},{8,24},{9,... | collective-permute-start | bytes 589832 | tf_op jit(solution)/shard_map/ppermute | solution.py:595
  139.9 13.5 %collective-permute-start.47 = (bf16[2,2,64,512]{3,2,1,0:T(8,128)(2,1)S(1)}, bf16[2,2,64,512]{3,2,1,0:T(8,128)(2,1)S(1)}, u32[]{:S(2)}, u32[]{:S(2)}) collective-permute-start(bf16[2,2,64,512]{3,2,1,0:T(8,128)(2,1)S(1)} %bitcast_dynamic-update-slice_fusion.28), channel_id=1, source_target_pairs={{0,24},{1,25},{2,26},{3,27},{4,28},{5,29},{6,30},{7,31},{8,16},{9,... | collective-permute-start | bytes 786440 | tf_op jit(solution)/shard_map/ppermute | solution.py:595
  153.3 52.0 %collective-permute-start.41 = (bf16[2,2,2,2,16,2048]{5,4,3,2,1,0:T(8,128)(2,1)S(1)}, bf16[2,2,2,2,16,2048]{5,4,3,2,1,0:T(8,128)(2,1)S(1)}, u32[]{:S(2)}, u32[]{:S(2)}) collective-permute-start(bf16[2,2,2,2,16,2048]{5,4,3,2,1,0:T(8,128)(2,1)S(1)} %bitcast_dynamic-update-slice_fusion.15), channel_id=1, source_target_pairs={{0,4},{1,5},{2,6},{3,7},{4,0},{5,1},{6,2},{7,3},{8,12},{9,13},{10,... | collective-permute-start | bytes 3145736 | tf_op jit(solution)/shard_map/ppermute | solution.py:595
  153.8 51.4 %collective-permute-start.48 = (bf16[2,2,2,2,64,512]{5,4,3,2,1,0:T(8,128)(2,1)S(1)}, bf16[2,2,2,2,64,512]{5,4,3,2,1,0:T(8,128)(2,1)S(1)}, u32[]{:S(2)}, u32[]{:S(2)}) collective-permute-start(bf16[2,2,2,2,64,512]{5,4,3,2,1,0:T(8,128)(2,1)S(1)} %bitcast_dynamic-update-slice_fusion.11), channel_id=1, source_target_pairs={{0,4},{1,5},{2,6},{3,7},{4,0},{5,1},{6,2},{7,3},{8,12},{9,13},{10,... | collective-permute-start | bytes 3145736 | tf_op jit(solution)/shard_map/ppermute | solution.py:595
  329.0 189.4 %reduce-scatter.5.cloned.1.call-start = ((), (), s32[]{:S(2)}) async-start(), calls=%async_computation.3 | async-start | bytes 983040 | tf_op jit(solution)/shard_map/reduce_scatter | solution.py:678
  416.3 14.1 %collective-permute-start.63 = (bf16[2,2,2,2,64,512]{5,4,3,2,1,0:T(8,128)(2,1)}, bf16[2,2,2,2,64,512]{5,4,3,2,1,0:T(8,128)(2,1)}, u32[]{:S(2)}, u32[]{:S(2)}) collective-permute-start(bf16[2,2,2,2,64,512]{5,4,3,2,1,0:T(8,128)(2,1)} %dynamic-slice_bitcast_fusion), channel_id=1, source_target_pairs={{0,4},{1,5},{2,6},{3,7},{4,0},{5,1},{6,2},{7,3},{8,12},{9,13},{10,... | collective-permute-start | bytes 3145736 | tf_op jit(solution)/shard_map/ppermute | solution.py:595
  433.1 14.7 %collective-permute-start.66 = (bf16[2,2,64,512]{3,2,1,0:T(8,128)(2,1)S(1)}, bf16[2,2,64,512]{3,2,1,0:T(8,128)(2,1)S(1)}, u32[]{:S(2)}, u32[]{:S(2)}) collective-permute-start(bf16[2,2,64,512]{3,2,1,0:T(8,128)(2,1)S(1)} %get-tuple-element.117), channel_id=1, source_target_pairs={{0,24},{1,25},{2,26},{3,27},{4,28},{5,29},{6,30},{7,31},{8,16},{9,... | collective-permute-start | bytes 786440 | tf_op jit(solution)/shard_map/ppermute | solution.py:595
  435.0 13.9 %collective-permute-start.65 = (bf16[2,2,64,512]{3,2,1,0:T(8,128)(2,1)S(1)}, bf16[2,2,64,512]{3,2,1,0:T(8,128)(2,1)S(1)}, u32[]{:S(2)}, u32[]{:S(2)}) collective-permute-start(bf16[2,2,64,512]{3,2,1,0:T(8,128)(2,1)S(1)} %get-tuple-element.118), channel_id=1, source_target_pairs={{0,16},{1,17},{2,18},{3,19},{4,20},{5,21},{6,22},{7,23},{8,24},{9,... | collective-permute-start | bytes 786440 | tf_op jit(solution)/shard_map/ppermute | solution.py:595
  437.6 34.2 %collective-permute-start.57 = (bf16[2,2,16,2048]{3,2,1,0:T(8,128)(2,1)S(1)}, bf16[2,2,16,2048]{3,2,1,0:T(8,128)(2,1)S(1)}, u32[]{:S(2)}, u32[]{:S(2)}) collective-permute-start(bf16[2,2,16,2048]{3,2,1,0:T(8,128)(2,1)S(1)} %get-tuple-element.119), channel_id=1, source_target_pairs={{0,8},{1,9},{2,10},{3,11},{4,12},{5,13},{6,14},{7,15},{8,0},{9,1},... | collective-permute-start | bytes 786440 | tf_op jit(solution)/shard_map/ppermute | solution.py:595
  440.2 18.2 %collective-permute-start.71 = (bf16[4,2,2,16,512]{4,3,0,2,1:T(8,128)(2,1)S(1)}, bf16[4,2,2,16,512]{4,3,0,2,1:T(8,128)(2,1)S(1)}, u32[]{:S(2)}, u32[]{:S(2)}) collective-permute-start(bf16[4,2,2,16,512]{4,3,0,2,1:T(8,128)(2,1)S(1)} %get-tuple-element.113), channel_id=1, source_target_pairs={{0,8},{1,9},{2,10},{3,11},{4,12},{5,13},{6,14},{7,15},{8,0},{9,1},... | collective-permute-start | bytes 786440 | tf_op jit(solution)/shard_map/ppermute | solution.py:595
  443.3 29.7 %collective-permute-start.59 = (bf16[2,2,16,2048]{3,2,1,0:T(8,128)(2,1)S(1)}, bf16[2,2,16,2048]{3,2,1,0:T(8,128)(2,1)S(1)}, u32[]{:S(2)}, u32[]{:S(2)}) collective-permute-start(bf16[2,2,16,2048]{3,2,1,0:T(8,128)(2,1)S(1)} %get-tuple-element.120), channel_id=1, source_target_pairs={{0,24},{1,25},{2,26},{3,27},{4,28},{5,29},{6,30},{7,31},{8,16},{9,... | collective-permute-start | bytes 786440 | tf_op jit(solution)/shard_map/ppermute | solution.py:595
  447.8 21.4 %collective-permute-start.73 = (bf16[4,2,2,16,512]{4,3,0,2,1:T(8,128)(2,1)S(1)}, bf16[4,2,2,16,512]{4,3,0,2,1:T(8,128)(2,1)S(1)}, u32[]{:S(2)}, u32[]{:S(2)}) collective-permute-start(bf16[4,2,2,16,512]{4,3,0,2,1:T(8,128)(2,1)S(1)} %get-tuple-element.114), channel_id=1, source_target_pairs={{0,24},{1,25},{2,26},{3,27},{4,28},{5,29},{6,30},{7,31},{8,16},{9,... | collective-permute-start | bytes 786440 | tf_op jit(solution)/shard_map/ppermute | solution.py:595
  448.9 20.7 %collective-permute-start.72 = (bf16[4,2,2,16,512]{4,3,0,2,1:T(8,128)(2,1)S(1)}, bf16[4,2,2,16,512]{4,3,0,2,1:T(8,128)(2,1)S(1)}, u32[]{:S(2)}, u32[]{:S(2)}) collective-permute-start(bf16[4,2,2,16,512]{4,3,0,2,1:T(8,128)(2,1)S(1)} %get-tuple-element.115), channel_id=1, source_target_pairs={{0,16},{1,17},{2,18},{3,19},{4,20},{5,21},{6,22},{7,23},{8,24},{9,... | collective-permute-start | bytes 786440 | tf_op jit(solution)/shard_map/ppermute | solution.py:595
  458.4 16.7 %collective-permute-start.58 = (bf16[2,2,16,2048]{3,2,1,0:T(8,128)(2,1)S(1)}, bf16[2,2,16,2048]{3,2,1,0:T(8,128)(2,1)S(1)}, u32[]{:S(2)}, u32[]{:S(2)}) collective-permute-start(bf16[2,2,16,2048]{3,2,1,0:T(8,128)(2,1)S(1)} %get-tuple-element.121), channel_id=1, source_target_pairs={{0,16},{1,17},{2,18},{3,19},{4,20},{5,21},{6,22},{7,23},{8,24},{9,... | collective-permute-start | bytes 786440 | tf_op jit(solution)/shard_map/ppermute | solution.py:595
  469.6 12.8 %collective-permute-start.52 = (bf16[4,2,2,16,512]{4,3,0,2,1:T(8,128)(2,1)S(1)}, bf16[4,2,2,16,512]{4,3,0,2,1:T(8,128)(2,1)S(1)}, u32[]{:S(2)}, u32[]{:S(2)}) collective-permute-start(bf16[4,2,2,16,512]{4,3,0,2,1:T(8,128)(2,1)S(1)} %get-tuple-element.123), channel_id=1, source_target_pairs={{0,24},{1,25},{2,26},{3,27},{4,28},{5,29},{6,30},{7,31},{8,16},{9,... | collective-permute-start | bytes 786440 | tf_op jit(solution)/shard_map/ppermute | solution.py:595
  471.8 14.1 %collective-permute-start.51 = (bf16[4,2,2,16,512]{4,3,0,2,1:T(8,128)(2,1)S(1)}, bf16[4,2,2,16,512]{4,3,0,2,1:T(8,128)(2,1)S(1)}, u32[]{:S(2)}, u32[]{:S(2)}) collective-permute-start(bf16[4,2,2,16,512]{4,3,0,2,1:T(8,128)(2,1)S(1)} %get-tuple-element.124), channel_id=1, source_target_pairs={{0,16},{1,17},{2,18},{3,19},{4,20},{5,21},{6,22},{7,23},{8,24},{9,... | collective-permute-start | bytes 786440 | tf_op jit(solution)/shard_map/ppermute | solution.py:595
  473.0 13.9 %collective-permute-start.67 = (bf16[64,512]{1,0:T(8,128)(2,1)S(1)}, bf16[64,512]{1,0:T(8,128)(2,1)S(1)}, u32[]{:S(2)}, u32[]{:S(2)}) collective-permute-start(bf16[64,512]{1,0:T(8,128)(2,1)S(1)} %get-tuple-element.128), channel_id=1, source_target_pairs={{0,1},{1,0},{2,3},{3,2},{4,5},{5,4},{6,7},{7,6},{8,9},{9,8},{10,11... | collective-permute-start | bytes 196616 | tf_op jit(solution)/shard_map/ppermute | solution.py:595
  482.4 35.1 %collective-permute-start.60 = (bf16[16,2048]{1,0:T(8,128)(2,1)S(1)}, bf16[16,2048]{1,0:T(8,128)(2,1)S(1)}, u32[]{:S(2)}, u32[]{:S(2)}) collective-permute-start(bf16[16,2048]{1,0:T(8,128)(2,1)S(1)} %get-tuple-element.131), channel_id=1, source_target_pairs={{0,1},{1,0},{2,3},{3,2},{4,5},{5,4},{6,7},{7,6},{8,9},{9,8},{10,11... | collective-permute-start | bytes 196616 | tf_op jit(solution)/shard_map/ppermute | solution.py:595
  485.9 31.6 %collective-permute-start.62 = (bf16[16,2048]{1,0:T(8,128)(2,1)S(1)}, bf16[16,2048]{1,0:T(8,128)(2,1)S(1)}, u32[]{:S(2)}, u32[]{:S(2)}) collective-permute-start(bf16[16,2048]{1,0:T(8,128)(2,1)S(1)} %get-tuple-element.132), channel_id=1, source_target_pairs={{0,3},{1,2},{2,1},{3,0},{4,7},{5,6},{6,5},{7,4},{8,11},{9,10},{10,... | collective-permute-start | bytes 196616 | tf_op jit(solution)/shard_map/ppermute | solution.py:595
  490.1 14.6 %collective-permute-start.75 = (bf16[4,16,512]{2,1,0:T(8,128)(2,1)S(1)}, bf16[4,16,512]{2,1,0:T(8,128)(2,1)S(1)}, u32[]{:S(2)}, u32[]{:S(2)}) collective-permute-start(bf16[4,16,512]{2,1,0:T(8,128)(2,1)S(1)} %get-tuple-element.127), channel_id=1, source_target_pairs={{0,2},{1,3},{2,0},{3,1},{4,6},{5,7},{6,4},{7,5},{8,10},{9,11},{10,... | collective-permute-start | bytes 196616 | tf_op jit(solution)/shard_map/ppermute | solution.py:595
  491.6 13.9 %collective-permute-start.53 = (bf16[4,16,512]{2,1,0:T(8,128)(2,1)S(1)}, bf16[4,16,512]{2,1,0:T(8,128)(2,1)S(1)}, u32[]{:S(2)}, u32[]{:S(2)}) collective-permute-start(bf16[4,16,512]{2,1,0:T(8,128)(2,1)S(1)} %get-tuple-element.134), channel_id=1, source_target_pairs={{0,1},{1,0},{2,3},{3,2},{4,5},{5,4},{6,7},{7,6},{8,9},{9,8},{10,11... | collective-permute-start | bytes 196616 | tf_op jit(solution)/shard_map/ppermute | solution.py:595
  495.1 13.3 %collective-permute-start.55 = (bf16[4,16,512]{2,1,0:T(8,128)(2,1)S(1)}, bf16[4,16,512]{2,1,0:T(8,128)(2,1)S(1)}, u32[]{:S(2)}, u32[]{:S(2)}) collective-permute-start(bf16[4,16,512]{2,1,0:T(8,128)(2,1)S(1)} %get-tuple-element.135), channel_id=1, source_target_pairs={{0,3},{1,2},{2,1},{3,0},{4,7},{5,6},{6,5},{7,4},{8,11},{9,10},{10,... | collective-permute-start | bytes 196616 | tf_op jit(solution)/shard_map/ppermute | solution.py:595
  505.4 12.2 %collective-permute-start.61 = (bf16[16,2048]{1,0:T(8,128)(2,1)S(1)}, bf16[16,2048]{1,0:T(8,128)(2,1)S(1)}, u32[]{:S(2)}, u32[]{:S(2)}) collective-permute-start(bf16[16,2048]{1,0:T(8,128)(2,1)S(1)} %get-tuple-element.133), channel_id=1, source_target_pairs={{0,2},{1,3},{2,0},{3,1},{4,6},{5,7},{6,4},{7,5},{8,10},{9,11},{10,... | collective-permute-start | bytes 196616 | tf_op jit(solution)/shard_map/ppermute | solution.py:595
  (92 other events, 906.8 us)
Sparse Core Ops, SparseCore 0:
  20.2 79.7 all-gather.2
  329.2 58.1 reduce-scatter.2
  487.0 31.4 reduce-scatter.4
